TPU v7x, 128 devices: a whole 4x4x4 slice. The times are simulated.
128 devices in a mesh: gx: 16 (over z, y), gy: 8 (over x, core).
Axes of the slice: x: 4, y: 4, z: 4, core: 2. Of those that a mesh axis runs over, the one named last changes fastest.
Arguments:
- tiles: float32 [16, 8, 2, 40, 40, 128], P('gx', 'gy'), may hold values from 0.25 to 4
- shifts: int32 [16, 8, 2], P('gx', 'gy'), may hold values from -4 to 4
- extents: int32 [16, 8, 4], P('gx', 'gy'), may hold values from 4 to 12
- conv1_weight: bfloat16 [3, 3, 3, 2, 32], replicated, may hold values from -0.875 to 0.875
- conv1_bias: float32 [32], replicated, may hold values from -3 to 3
- conv2_weight: bfloat16 [3, 3, 3, 32, 32], replicated, may hold values from -0.21875 to 0.21875
- conv2_bias: float32 [32], replicated, may hold values from -3 to 3
- head_weight: bfloat16 [32, 2], replicated, may hold values from -1 to 1
- head_bias: float32 [2], replicated, may hold values from -3 to 3
Outputs:
- joined: float32 [2, 256, 128, 128], P(None, 'gx', 'gy')
- restored: float32 [2, 256, 128, 128], P(None, 'gx', 'gy')
All inputs are finite; a program needn't handle non-finite values.
Results may differ from a plain program's by a relative error of at most 0.0057.
Values may be sent and summed in bfloat16 or wider, within the bound.
A program may use at most 64 MiB of HBM per device.

v0:
```python
import jax
import jax.numpy as jnp
from jax import lax
from jax.sharding import PartitionSpec as P

MARGIN = 12
SHIFT = 4
RAMP = 8


def shifted(block, axis, distance):
    devices = range(lax.axis_size(axis))
    route = [(i - distance, i) for i in devices if i - distance in devices]
    return lax.ppermute(block, axis, route)


def padded(cells, sides, width):
    for axis, dim in sides:
        count = lax.axis_size(axis)
        ends = count - 1
        head = lax.slice_in_dim(cells, 0, width, axis=dim)
        tail = lax.slice_in_dim(cells, cells.shape[dim] - width, cells.shape[dim], axis=dim)
        cells = jnp.concatenate(
            [
                lax.ppermute(tail, axis, [(i, (i + 1) % count) for i in range(ends)]),
                cells,
                lax.ppermute(head, axis, [((i + 1) % count, i) for i in range(ends)]),
            ],
            axis=dim,
        )
    return cells


def feather(low, high, length):
    places = jnp.arange(length, dtype=jnp.int32)
    inside = (places >= low) & (places < high)
    ramped = jnp.minimum(jnp.minimum(places - low + 1, high - places), RAMP)
    return jnp.where(inside, ramped.astype(jnp.float32), jnp.float32(0.0)) / RAMP


def pad_axis(values, axis, before, after):
    widths = [(0, 0)] * values.ndim
    widths[axis] = (before, after)
    return values


def rows_across(strip_pair, offset):
    return shifted(strip_pair, "gx", offset)


def cols_across(strip_pair, offset):
    return shifted(strip_pair, "gy", offset)


def fold_edges(canvas_sum, canvas_wts, extent, rim_width, mover, axis):
    from_after = mover(
        (
            lax.slice_in_dim(canvas_sum, 0, rim_width, axis=axis),
            lax.slice_in_dim(canvas_wts, 0, rim_width, axis=axis - 1),
        ),
        -1,
    )
    from_before = mover(
        (
            lax.slice_in_dim(canvas_sum, extent + rim_width, extent + 2 * rim_width, axis=axis),
            lax.slice_in_dim(canvas_wts, extent + rim_width, extent + 2 * rim_width, axis=axis - 1),
        ),
        1,
    )
    core_sum = lax.slice_in_dim(canvas_sum, rim_width, rim_width + extent, axis=axis)
    core_sum = (
        core_sum
        + pad_axis(from_before[0], axis, 0, extent - rim_width)
        + pad_axis(from_after[0], axis, extent - rim_width, 0)
    )
    core_wts = lax.slice_in_dim(canvas_wts, rim_width, rim_width + extent, axis=axis - 1)
    core_wts = (
        core_wts
        + pad_axis(from_before[1], axis - 1, 0, extent - rim_width)
        + pad_axis(from_after[1], axis - 1, extent - rim_width, 0)
    )
    return (core_sum, core_wts)


def conv_rows(source, weight, bias):
    in_width = source.shape[0]
    out_rows = source.shape[1] - 2
    out_cols = source.shape[2] - 2
    planes = source.shape[3]
    out_width = weight.shape[4]
    all_taps = 27 * in_width <= 256
    depth_padded = jnp.pad(source, ((0, 0), (0, 0), (0, 0), (1, 1)))
    stack_width = 27 * in_width if all_taps else 9 * in_width
    block_limit = 8 * 1024 * 1024 // (stack_width * out_cols * planes * 2 + 1)
    block_rows_max = max(1, min(out_rows, block_limit))
    flat_all = weight.reshape(27 * in_width, out_width)
    flat_rows = weight.reshape(3, 9 * in_width, out_width)
    blocks = []
    for first_row in range(0, out_rows, block_rows_max):
        block_rows = min(block_rows_max, out_rows - first_row)
        window = depth_padded[:, first_row : first_row + block_rows + 2]
        if all_taps:
            pieces = []
            for row_tap in range(3):
                for col_tap in range(3):
                    for depth_tap in range(3):
                        pieces.append(
                            window[
                                :,
                                row_tap : row_tap + block_rows,
                                col_tap : col_tap + out_cols,
                                depth_tap : depth_tap + planes,
                            ]
                        )
            stacked = jnp.concatenate(pieces, axis=0)
            summed = jnp.einsum(
                "ko,krcz->orcz", flat_all, stacked, preferred_element_type=jnp.float32
            )
        else:
            pieces = []
            for col_tap in range(3):
                for depth_tap in range(3):
                    pieces.append(
                        window[:, :, col_tap : col_tap + out_cols, depth_tap : depth_tap + planes]
                    )
            stacked = jnp.concatenate(pieces, axis=0)
            summed = jnp.zeros((out_width, block_rows, out_cols, planes), jnp.float32)
            for row_tap in range(3):
                summed = summed + jnp.einsum(
                    "ko,krcz->orcz",
                    flat_rows[row_tap],
                    stacked[:, row_tap : row_tap + block_rows],
                    preferred_element_type=jnp.float32,
                )
        blocks.append(summed)
    return jax.nn.relu(jnp.concatenate(blocks, axis=1) + bias[:, None, None, None])


def shards(
    tiles,
    shifts,
    extents,
    conv1_weight,
    conv1_bias,
    conv2_weight,
    conv2_bias,
    head_weight,
    head_bias,
):
    own_tile = tiles[0, 0]
    offsets = shifts[0, 0]
    margins = extents[0, 0]
    channels = own_tile.shape[0]
    tile_height = own_tile.shape[1]
    tile_width = own_tile.shape[2]
    planes = own_tile.shape[3]
    slab_rows = tile_height - 2 * MARGIN
    slab_cols = tile_width - 2 * MARGIN
    rim_width = MARGIN + SHIFT
    weight = (
        feather(MARGIN - margins[0], MARGIN + slab_rows + margins[1], tile_height)[:, None]
        * feather(MARGIN - margins[2], MARGIN + slab_cols + margins[3], tile_width)[None, :]
    )
    canvas_sum = jnp.zeros(
        (channels, slab_rows + 2 * rim_width, slab_cols + 2 * rim_width, planes), jnp.float32
    )
    canvas_wts = jnp.zeros((slab_rows + 2 * rim_width, slab_cols + 2 * rim_width), jnp.float32)
    top_row = SHIFT + offsets[0]
    left_col = SHIFT + offsets[1]
    zero_index = jnp.int32(0)
    canvas_sum = lax.dynamic_update_slice(
        canvas_sum, own_tile * weight[None, :, :, None], (zero_index, top_row, left_col, zero_index)
    )
    canvas_wts = lax.dynamic_update_slice(canvas_wts, weight, (top_row, left_col))
    row_sum, row_wts = fold_edges(canvas_sum, canvas_wts, slab_rows, rim_width, rows_across, 1)
    core_sum, core_wts = fold_edges(row_sum, row_wts, slab_cols, rim_width, cols_across, 2)
    joined = core_sum / core_wts[None, :, :, None]
    joined_low = joined.astype(jnp.bfloat16)
    padded_image = padded(joined_low, (("gx", 1), ("gy", 2)), 1)
    first_act = conv_rows(padded_image, conv1_weight, conv1_bias).astype(jnp.bfloat16)
    bordered = padded(first_act, (("gx", 1), ("gy", 2)), 1)
    second = conv_rows(bordered, conv2_weight, conv2_bias).astype(jnp.bfloat16)
    restored = (
        jnp.einsum("oc,orxz->crxz", head_weight, second, preferred_element_type=jnp.float32)
        + head_bias[:, None, None, None]
    )
    return (joined, restored)


def solution(mesh):
    return jax.shard_map(
        shards,
        mesh=mesh,
        in_specs=(
            P("gx", "gy", None, None, None, None),
            P("gx", "gy", None),
            P("gx", "gy", None),
            P(),
            P(),
            P(),
            P(),
            P(),
            P(),
        ),
        out_specs=(P(None, "gx", "gy", None), P(None, "gx", "gy", None)),
        check_vma=False,
    )
```

profile of v0, /device:TPU:1, one launch (start us, length us, event | category | flops | bytes accessed | tf_op | source)
XLA Modules:
  0.0 149.6 jit_solution(4611636967162327883)
XLA Ops:
  0.6 1.3 fusion.50
  4.5 1.5 fusion.51
  8.7 1.1 broadcast_in_dim.9
  9.8 4.7 %fusion.10 = f32[2,48,48,128]{3,0,2,1:T(2,128)S(1)} fusion(f32[2,48,48,128]{3,0,2,1:T(2,128)S(1)} %broadcast_in_dim.9, s32[]{:T(128)S(6)} %select_n.25, s32[]{:T(128)S(6)} %select_n.26, f32[1,1,2,40,40,128]{5,4,3,2,1,0:T(8,128)} %param.9, f32[40,40]{1,0:T(8,128)S(1)} %broadcast_multiply_fusion), kind=kLoop, calls=%fused_computation.20 | loop fusion | flops 409600 | bytes 3297288 | tf_op jit(solution)/shard_map/dynamic_update_slice | solution.py:171
  14.5 1.3 fusion.40
  15.8 4.0 %collective-permute-start = (f32[2,16,48,128]{3,0,2,1:T(2,128)}, f32[2,16,48,128]{3,0,2,1:T(2,128)S(1)}, u32[]{:S(2)}, u32[]{:S(2)}) collective-permute-start(f32[2,16,48,128]{3,0,2,1:T(2,128)} %get-tuple-element.28), channel_id=1, source_target_pairs={{0,8},{8,16},{16,24},{24,32},{32,40},{40,48},{48,56},{56,64},{64,7... | collective-permute-start | bytes 2359304 | tf_op jit(solution)/shard_map/ppermute | solution.py:14
  19.8 1.3 collective-permute-start.1
  21.1 1.0 dynamic_update_slice.7
  22.1 4.0 %collective-permute-start.4 = (f32[16,48]{1,0:T(8,128)S(1)}, f32[16,48]{1,0:T(8,128)S(1)}, u32[]{:S(2)}, u32[]{:S(2)}) collective-permute-start(f32[16,48]{1,0:T(8,128)S(1)} %get-tuple-element.71), channel_id=1, source_target_pairs={{0,8},{8,16},{16,24},{24,32},{32,40},{40,48},{48,56},{56,64},{64,7... | collective-permute-start | bytes 9224 | tf_op jit(solution)/shard_map/ppermute | solution.py:14
  26.1 1.3 collective-permute-start.5
  27.4 8.9 %collective-permute-done.4 = f32[16,48]{1,0:T(8,128)S(1)} collective-permute-done((f32[16,48]{1,0:T(8,128)S(1)}, f32[16,48]{1,0:T(8,128)S(1)}, u32[]{:S(2)}, u32[]{:S(2)}) %collective-permute-start.4) | collective-permute-done | bytes 3104 | tf_op jit(solution)/shard_map/ppermute | solution.py:14
  36.3 3.9 %collective-permute-done.5 = f32[16,48]{1,0:T(8,128)S(1)} collective-permute-done((f32[16,48]{1,0:T(8,128)S(1)}, f32[16,48]{1,0:T(8,128)S(1)}, u32[]{:S(2)}, u32[]{:S(2)}) %collective-permute-start.5) | collective-permute-done | bytes 3104 | tf_op jit(solution)/shard_map/ppermute | solution.py:14
  40.3 2.1 %fusion.21 = f32[2,16,48,128]{3,0,2,1:T(2,128)S(1)} fusion(f32[2,16,48,128]{3,0,2,1:T(2,128)} %collective-permute-done.1, f32[2,16,48,128]{3,0,2,1:T(2,128)S(1)} %collective-permute-done, f32[2,48,48,128]{3,0,2,1:T(2,128)S(1)} %fusion.10), kind=kLoop, calls=%fused_computation.48 | loop fusion | flops 393216 | bytes 3145728 | tf_op jit(solution)/shard_map/add | solution.py:72
  42.4 4.8 %collective-permute-start.2 = (f32[2,16,16,128]{3,0,2,1:T(2,128)S(1)}, f32[2,16,16,128]{3,0,2,1:T(2,128)S(1)}, u32[]{:S(2)}, u32[]{:S(2)}) collective-permute-start(f32[2,16,16,128]{3,0,2,1:T(2,128)S(1)} %get-tuple-element.34), channel_id=1, source_target_pairs={{0,1},{1,2},{2,3},{3,4},{4,5},{5,6},{6,7},{8,9},{9,10},{10,11},{11... | collective-permute-start | bytes 786440 | tf_op jit(solution)/shard_map/ppermute | solution.py:14
  47.2 1.9 %collective-permute-start.3 = (f32[2,16,16,128]{3,0,2,1:T(2,128)S(1)}, f32[2,16,16,128]{3,0,2,1:T(2,128)S(1)}, u32[]{:S(2)}, u32[]{:S(2)}) collective-permute-start(f32[2,16,16,128]{3,0,2,1:T(2,128)S(1)} %get-tuple-element.35), channel_id=1, source_target_pairs={{1,0},{2,1},{3,2},{4,3},{5,4},{6,5},{7,6},{9,8},{10,9},{11,10},{12... | collective-permute-start | bytes 786440 | tf_op jit(solution)/shard_map/ppermute | solution.py:14
  49.2 3.6 %collective-permute-start.6 = (f32[16,16]{1,0:T(8,128)S(1)}, f32[16,16]{1,0:T(8,128)S(1)}, u32[]{:S(2)}, u32[]{:S(2)}) collective-permute-start(f32[16,16]{1,0:T(8,128)S(1)} %get-tuple-element.73), channel_id=1, source_target_pairs={{0,1},{1,2},{2,3},{3,4},{4,5},{5,6},{6,7},{8,9},{9,10},{10,11},{11... | collective-permute-start | bytes 3080 | tf_op jit(solution)/shard_map/ppermute | solution.py:14
  52.9 1.9 %collective-permute-start.7 = (f32[16,16]{1,0:T(8,128)S(1)}, f32[16,16]{1,0:T(8,128)S(1)}, u32[]{:S(2)}, u32[]{:S(2)}) collective-permute-start(f32[16,16]{1,0:T(8,128)S(1)} %get-tuple-element.74), channel_id=1, source_target_pairs={{1,0},{2,1},{3,2},{4,3},{5,4},{6,5},{7,6},{9,8},{10,9},{11,10},{12... | collective-permute-start | bytes 3080 | tf_op jit(solution)/shard_map/ppermute | solution.py:14
  54.8 3.0 %collective-permute-done.7 = f32[16,16]{1,0:T(8,128)S(1)} collective-permute-done((f32[16,16]{1,0:T(8,128)S(1)}, f32[16,16]{1,0:T(8,128)S(1)}, u32[]{:S(2)}, u32[]{:S(2)}) %collective-permute-start.7) | collective-permute-done | bytes 1056 | tf_op jit(solution)/shard_map/ppermute | solution.py:14
  58.4 3.1 %collective-permute-start.8 = (bf16[2,1,16,128]{3,0,2,1:T(2,128)(2,1)S(1)}, bf16[2,1,16,128]{3,0,2,1:T(2,128)(2,1)S(1)}, u32[]{:S(2)}, u32[]{:S(2)}) collective-permute-start(bf16[2,1,16,128]{3,0,2,1:T(2,128)(2,1)S(1)} %get-tuple-element.69), channel_id=1, source_target_pairs={{0,8},{8,16},{16,24},{24,32},{32,40},{40,48},{48,56},{56,64},{64,7... | collective-permute-start | bytes 24584 | tf_op jit(solution)/shard_map/ppermute | solution.py:25
  61.5 1.3 collective-permute-start.9
  63.5 2.5 %collective-permute-done.9 = bf16[2,1,16,128]{3,0,2,1:T(2,128)(2,1)S(1)} collective-permute-done((bf16[2,1,16,128]{3,0,2,1:T(2,128)(2,1)S(1)}, bf16[2,1,16,128]{3,0,2,1:T(2,128)(2,1)S(1)}, u32[]{:S(2)}, u32[]{:S(2)}) %collective-permute-start.9) | collective-permute-done | bytes 8224 | tf_op jit(solution)/shard_map/ppermute | solution.py:27
  66.0 3.4 %collective-permute-start.10 = (bf16[2,18,1,128]{3,0,2,1:T(2,128)(2,1)S(1)}, bf16[2,18,1,128]{3,0,2,1:T(2,128)(2,1)S(1)}, u32[]{:S(2)}, u32[]{:S(2)}) collective-permute-start(bf16[2,18,1,128]{3,0,2,1:T(2,128)(2,1)S(1)} %get-tuple-element.65), channel_id=1, source_target_pairs={{0,1},{1,2},{2,3},{3,4},{4,5},{5,6},{6,7},{8,9},{9,10},{10,11},{11... | collective-permute-start | bytes 27656 | tf_op jit(solution)/shard_map/ppermute | solution.py:25
  69.4 1.9 %collective-permute-start.11 = (bf16[2,18,1,128]{3,0,2,1:T(2,128)(2,1)S(1)}, bf16[2,18,1,128]{3,0,2,1:T(2,128)(2,1)S(1)}, u32[]{:S(2)}, u32[]{:S(2)}) collective-permute-start(bf16[2,18,1,128]{3,0,2,1:T(2,128)(2,1)S(1)} %get-tuple-element.66), channel_id=1, source_target_pairs={{1,0},{2,1},{3,2},{4,3},{5,4},{6,5},{7,6},{9,8},{10,9},{11,10},{12... | collective-permute-start | bytes 27656 | tf_op jit(solution)/shard_map/ppermute | solution.py:27
  71.5 2.8 %collective-permute-done.11 = bf16[2,18,1,128]{3,0,2,1:T(2,128)(2,1)S(1)} collective-permute-done((bf16[2,18,1,128]{3,0,2,1:T(2,128)(2,1)S(1)}, bf16[2,18,1,128]{3,0,2,1:T(2,128)(2,1)S(1)}, u32[]{:S(2)}, u32[]{:S(2)}) %collective-permute-start.11) | collective-permute-done | bytes 9248 | tf_op jit(solution)/shard_map/ppermute | solution.py:27
  75.0 0.9 fusion.46
  75.9 0.8 select_maximum_fusion.2
  76.7 2.5 %fusion.43 = (bf16[2,16,16,128]{3,0,2,1:T(2,128)(2,1)S(1)}, bf16[2,16,16,128]{3,0,2,1:T(2,128)(2,1)S(1)}, bf16[2,16,16,128]{3,0,2,1:T(2,128)(2,1)S(1)}, bf16[2,1...) fusion(bf16[2,18,18,130]{3,0,2,1:T(2,128)(2,1)S(1)} %select_max, ...), kind=kLoop, calls=%fused_computation.96 | loop fusion | bytes 4718592 | tf_op jit(solution)/shard_map/slice | solution.py:108
  79.3 16.1 %concatenate.65 = bf16[54,16,16,128]{3,0,2,1:T(8,128)(2,1)} concatenate(bf16[2,16,16,128]{3,0,2,1:T(2,128)(2,1)S(1)} %get-tuple-element.53, bf16[2,16,16,128]{3,0,2,1:T(2,128)(2,1)} %get-tuple-element.62, bf16[2,16,16,128]{3,0,2,1:T(2,128)(2,1)S(1)} %get-tuple-element.52, bf16[2,16,16,128]{3,0,2,1:T(2,128)(2,1)S(1)} %get-tuple-element.51, ...), dimensions={0} | concatenate | bytes 7077888 | tf_op jit(solution)/shard_map/concatenate | solution.py:115
  95.4 2.8 %fusion.11 = bf16[32,16,16,128]{3,0,2,1:T(8,128)(2,1)S(1)} fusion(f32[32]{0:T(128)S(1)} %copy-done.4, bf16[54,16,16,128]{3,0,2,1:T(8,128)(2,1)} %concatenate.65, bf16[54,32]{1,0:T(8,128)(2,1)} %reshape.111), kind=kOutput, calls=%fused_computation.21 | convolution fusion | flops 116391936 | bytes 5639680 | tf_op jit(solution)/shard_map/ko,krcz->orcz/dot_general | solution.py:116
  98.3 4.6 %collective-permute-start.12 = (bf16[32,1,16,128]{3,0,2,1:T(8,128)(2,1)S(1)}, bf16[32,1,16,128]{3,0,2,1:T(8,128)(2,1)S(1)}, u32[]{:S(2)}, u32[]{:S(2)}) collective-permute-start(bf16[32,1,16,128]{3,0,2,1:T(8,128)(2,1)S(1)} %get-tuple-element.32), channel_id=1, source_target_pairs={{0,8},{8,16},{16,24},{24,32},{32,40},{40,48},{48,56},{56,64},{64,7... | collective-permute-start | bytes 393224 | tf_op jit(solution)/shard_map/ppermute | solution.py:25
  102.9 1.3 collective-permute-start.13
  104.8 4.1 %collective-permute-done.13 = bf16[32,1,16,128]{3,0,2,1:T(8,128)(2,1)S(1)} collective-permute-done((bf16[32,1,16,128]{3,0,2,1:T(8,128)(2,1)S(1)}, bf16[32,1,16,128]{3,0,2,1:T(8,128)(2,1)S(1)}, u32[]{:S(2)}, u32[]{:S(2)}) %collective-permute-start.13) | collective-permute-done | bytes 131104 | tf_op jit(solution)/shard_map/ppermute | solution.py:27
  108.9 4.0 %collective-permute-start.14 = (bf16[32,18,1,128]{3,0,2,1:T(8,128)(2,1)S(1)}, bf16[32,18,1,128]{3,0,2,1:T(8,128)(2,1)S(1)}, u32[]{:S(2)}, u32[]{:S(2)}) collective-permute-start(bf16[32,18,1,128]{3,0,2,1:T(8,128)(2,1)S(1)} %get-tuple-element.26), channel_id=1, source_target_pairs={{0,1},{1,2},{2,3},{3,4},{4,5},{5,6},{6,7},{8,9},{9,10},{10,11},{11... | collective-permute-start | bytes 442376 | tf_op jit(solution)/shard_map/ppermute | solution.py:25
  112.9 1.9 %collective-permute-start.15 = (bf16[32,18,1,128]{3,0,2,1:T(8,128)(2,1)S(1)}, bf16[32,18,1,128]{3,0,2,1:T(8,128)(2,1)S(1)}, u32[]{:S(2)}, u32[]{:S(2)}) collective-permute-start(bf16[32,18,1,128]{3,0,2,1:T(8,128)(2,1)S(1)} %get-tuple-element.27), channel_id=1, source_target_pairs={{1,0},{2,1},{3,2},{4,3},{5,4},{6,5},{7,6},{9,8},{10,9},{11,10},{12... | collective-permute-start | bytes 442376 | tf_op jit(solution)/shard_map/ppermute | solution.py:27
  115.6 3.8 %collective-permute-done.15 = bf16[32,18,1,128]{3,0,2,1:T(8,128)(2,1)S(1)} collective-permute-done((bf16[32,18,1,128]{3,0,2,1:T(8,128)(2,1)S(1)}, bf16[32,18,1,128]{3,0,2,1:T(8,128)(2,1)S(1)}, u32[]{:S(2)}, u32[]{:S(2)}) %collective-permute-start.15) | collective-permute-done | bytes 147488 | tf_op jit(solution)/shard_map/ppermute | solution.py:27
  119.4 5.0 %select_maximum_fusion = bf16[32,18,18,130]{3,0,2,1:T(8,128)(2,1)S(1)} fusion(bf16[32,18,1,128]{3,0,2,1:T(8,128)(2,1)S(1)} %collective-permute-done.15, bf16[32,18,1,128]{3,0,2,1:T(8,128)(2,1)S(1)} %collective-permute-done.14, bf16[32,1,16,128]{3,0,2,1:T(8,128)(2,1)S(1)} %collective-permute-done.13, bf16[32,16,16,128]{3,0,2,1:T(8,128)(2,1)S(1)} %fusion.11, ...), kind=kLoop, calls=%fused_computation.3 | loop fusion | flops 24261120 | bytes 5349888 | tf_op jit(solution)/shard_map/concatenate | solution.py:23
  124.9 1.1 pad_maximum_fusion
  125.9 0.7 slice_dynamic-update-slice_fusion.15
  126.7 1.4 slice_dynamic-update-slice_fusion.14
  129.4 1.4 slice_dynamic-update-slice_fusion.12
  132.3 1.4 slice_dynamic-update-slice_fusion.9
  133.7 1.6 %fusion.52 = f32[7,16,128,32]{2,3,1,0:T(8,128)S(1)} fusion(bf16[288,9,16,128]{3,0,2,1:T(8,128)(2,1)S(1)} %get-tuple-element.8, bf16[288,32,1,1]{1,0,3,2:T(8,128)(2,1)S(1)} %bitcast.70), kind=kOutput, calls=%fused_computation.105 | convolution fusion | flops 264241152 | bytes 12470272 | tf_op jit(solution)/shard_map/ko,krcz->orcz/dot_general | solution.py:129
  135.3 2.9 %fusion.53 = f32[7,16,128,32]{2,3,1,0:T(8,128)} fusion(bf16[288,9,16,128]{3,0,2,1:T(8,128)(2,1)S(1)} %get-tuple-element.8, bf16[288,32,1,1]{1,0,3,2:T(8,128)(2,1)S(1)} %bitcast.67), kind=kOutput, calls=%fused_computation.106 | convolution fusion | flops 264241152 | bytes 12470272 | tf_op jit(solution)/shard_map/ko,krcz->orcz/dot_general | solution.py:129
  138.2 1.6 %fusion.55 = f32[7,16,128,32]{2,3,1,0:T(8,128)S(1)} fusion(bf16[288,9,16,128]{3,0,2,1:T(8,128)(2,1)S(1)} %get-tuple-element.9, bf16[288,32,1,1]{1,0,3,2:T(8,128)(2,1)S(1)} %bitcast.68), kind=kOutput, calls=%fused_computation.108 | convolution fusion | flops 264241152 | bytes 12470272 | tf_op jit(solution)/shard_map/ko,krcz->orcz/dot_general | solution.py:129
  139.8 1.6 %fusion.54 = f32[7,16,128,32]{2,3,1,0:T(8,128)S(1)} fusion(bf16[288,9,16,128]{3,0,2,1:T(8,128)(2,1)S(1)} %get-tuple-element.9, bf16[288,32,1,1]{1,0,3,2:T(8,128)(2,1)S(1)} %bitcast.71), kind=kOutput, calls=%fused_computation.107 | convolution fusion | flops 264241152 | bytes 12470272 | tf_op jit(solution)/shard_map/ko,krcz->orcz/dot_general | solution.py:129
  143.0 0.8 fusion.56
  144.4 1.7 %add_bitcast_fusion.1 = f32[32,7,16,128]{3,0,2,1:T(8,128)S(1)} fusion(f32[7,16,128,32]{2,3,1,0:T(8,128)S(1)} %fusion.52, f32[7,16,128,32]{2,3,1,0:T(8,128)S(1)} %copy-done.1, bf16[288,9,16,128]{3,0,2,1:T(8,128)(2,1)S(1)} %get-tuple-element.8, bf16[288,32,1,1]{1,0,3,2:T(8,128)(2,1)S(1)} %bitcast.65), kind=kOutput, calls=%fused_computation.18 | convolution fusion | flops 265158656 | bytes 16140288 | tf_op jit(solution)/shard_map/ko,krcz->orcz/dot_general | solution.py:129
  146.1 1.6 %add_bitcast_fusion = f32[32,7,16,128]{3,0,2,1:T(8,128)S(1)} fusion(f32[7,16,128,32]{2,3,1,0:T(8,128)S(1)} %fusion.54, f32[7,16,128,32]{2,3,1,0:T(8,128)S(1)} %fusion.55, bf16[288,9,16,128]{3,0,2,1:T(8,128)(2,1)S(1)} %get-tuple-element.9, bf16[288,32,1,1]{1,0,3,2:T(8,128)(2,1)S(1)} %bitcast.66), kind=kOutput, calls=%fused_computation.17 | convolution fusion | flops 265158656 | bytes 16140288 | tf_op jit(solution)/shard_map/ko,krcz->orcz/dot_general | solution.py:129
  (60 shorter events, 11.0 us)
Async XLA Ops:
  0.6 147.7 %copy-start = (bf16[32,2]{0,1:T(2,128)(2,1)S(1)}, bf16[32,2]{0,1:T(2,128)(2,1)}, u32[]{:S(2)}) copy-start(bf16[32,2]{0,1:T(2,128)(2,1)} %param.16) | copy-start | bytes 388
  14.5 48.4 %copy-start.3 = (bf16[3,3,3,2,32]{4,3,2,1,0:T(2,128)(2,1)S(1)}, bf16[3,3,3,2,32]{4,3,2,1,0:T(2,128)(2,1)}, u32[]{:S(2)}) copy-start(bf16[3,3,3,2,32]{4,3,2,1,0:T(2,128)(2,1)} %param.12) | copy-start | bytes 10372
  15.8 24.5 %collective-permute-start = (f32[2,16,48,128]{3,0,2,1:T(2,128)}, f32[2,16,48,128]{3,0,2,1:T(2,128)S(1)}, u32[]{:S(2)}, u32[]{:S(2)}) collective-permute-start(f32[2,16,48,128]{3,0,2,1:T(2,128)} %get-tuple-element.28), channel_id=1, source_target_pairs={{0,8},{8,16},{16,24},{24,32},{32,40},{40,48},{48,56},{56,64},{64,7... | collective-permute-start | bytes 2359304 | tf_op jit(solution)/shard_map/ppermute | solution.py:14
  19.8 20.5 %collective-permute-start.1 = (f32[2,16,48,128]{3,0,2,1:T(2,128)}, f32[2,16,48,128]{3,0,2,1:T(2,128)}, u32[]{:S(2)}, u32[]{:S(2)}) collective-permute-start(f32[2,16,48,128]{3,0,2,1:T(2,128)} %get-tuple-element.29), channel_id=1, source_target_pairs={{8,0},{16,8},{24,16},{32,24},{40,32},{48,40},{56,48},{64,56},{72,6... | collective-permute-start | bytes 2359304 | tf_op jit(solution)/shard_map/ppermute | solution.py:14
  22.1 14.2 %collective-permute-start.4 = (f32[16,48]{1,0:T(8,128)S(1)}, f32[16,48]{1,0:T(8,128)S(1)}, u32[]{:S(2)}, u32[]{:S(2)}) collective-permute-start(f32[16,48]{1,0:T(8,128)S(1)} %get-tuple-element.71), channel_id=1, source_target_pairs={{0,8},{8,16},{16,24},{24,32},{32,40},{40,48},{48,56},{56,64},{64,7... | collective-permute-start | bytes 9224 | tf_op jit(solution)/shard_map/ppermute | solution.py:14
  26.1 14.2 %collective-permute-start.5 = (f32[16,48]{1,0:T(8,128)S(1)}, f32[16,48]{1,0:T(8,128)S(1)}, u32[]{:S(2)}, u32[]{:S(2)}) collective-permute-start(f32[16,48]{1,0:T(8,128)S(1)} %get-tuple-element.72), channel_id=1, source_target_pairs={{8,0},{16,8},{24,16},{32,24},{40,32},{48,40},{56,48},{64,56},{72,6... | collective-permute-start | bytes 9224 | tf_op jit(solution)/shard_map/ppermute | solution.py:14
  42.4 15.5 %collective-permute-start.2 = (f32[2,16,16,128]{3,0,2,1:T(2,128)S(1)}, f32[2,16,16,128]{3,0,2,1:T(2,128)S(1)}, u32[]{:S(2)}, u32[]{:S(2)}) collective-permute-start(f32[2,16,16,128]{3,0,2,1:T(2,128)S(1)} %get-tuple-element.34), channel_id=1, source_target_pairs={{0,1},{1,2},{2,3},{3,4},{4,5},{5,6},{6,7},{8,9},{9,10},{10,11},{11... | collective-permute-start | bytes 786440 | tf_op jit(solution)/shard_map/ppermute | solution.py:14
  47.2 10.7 %collective-permute-start.3 = (f32[2,16,16,128]{3,0,2,1:T(2,128)S(1)}, f32[2,16,16,128]{3,0,2,1:T(2,128)S(1)}, u32[]{:S(2)}, u32[]{:S(2)}) collective-permute-start(f32[2,16,16,128]{3,0,2,1:T(2,128)S(1)} %get-tuple-element.35), channel_id=1, source_target_pairs={{1,0},{2,1},{3,2},{4,3},{5,4},{6,5},{7,6},{9,8},{10,9},{11,10},{12... | collective-permute-start | bytes 786440 | tf_op jit(solution)/shard_map/ppermute | solution.py:14
  49.2 5.6 %collective-permute-start.6 = (f32[16,16]{1,0:T(8,128)S(1)}, f32[16,16]{1,0:T(8,128)S(1)}, u32[]{:S(2)}, u32[]{:S(2)}) collective-permute-start(f32[16,16]{1,0:T(8,128)S(1)} %get-tuple-element.73), channel_id=1, source_target_pairs={{0,1},{1,2},{2,3},{3,4},{4,5},{5,6},{6,7},{8,9},{9,10},{10,11},{11... | collective-permute-start | bytes 3080 | tf_op jit(solution)/shard_map/ppermute | solution.py:14
  52.9 5.0 %collective-permute-start.7 = (f32[16,16]{1,0:T(8,128)S(1)}, f32[16,16]{1,0:T(8,128)S(1)}, u32[]{:S(2)}, u32[]{:S(2)}) collective-permute-start(f32[16,16]{1,0:T(8,128)S(1)} %get-tuple-element.74), channel_id=1, source_target_pairs={{1,0},{2,1},{3,2},{4,3},{5,4},{6,5},{7,6},{9,8},{10,9},{11,10},{12... | collective-permute-start | bytes 3080 | tf_op jit(solution)/shard_map/ppermute | solution.py:14
  58.4 5.1 %collective-permute-start.8 = (bf16[2,1,16,128]{3,0,2,1:T(2,128)(2,1)S(1)}, bf16[2,1,16,128]{3,0,2,1:T(2,128)(2,1)S(1)}, u32[]{:S(2)}, u32[]{:S(2)}) collective-permute-start(bf16[2,1,16,128]{3,0,2,1:T(2,128)(2,1)S(1)} %get-tuple-element.69), channel_id=1, source_target_pairs={{0,8},{8,16},{16,24},{24,32},{32,40},{40,48},{48,56},{56,64},{64,7... | collective-permute-start | bytes 24584 | tf_op jit(solution)/shard_map/ppermute | solution.py:25
  61.5 4.4 %collective-permute-start.9 = (bf16[2,1,16,128]{3,0,2,1:T(2,128)(2,1)S(1)}, bf16[2,1,16,128]{3,0,2,1:T(2,128)(2,1)S(1)}, u32[]{:S(2)}, u32[]{:S(2)}) collective-permute-start(bf16[2,1,16,128]{3,0,2,1:T(2,128)(2,1)S(1)} %get-tuple-element.70), channel_id=1, source_target_pairs={{8,0},{16,8},{24,16},{32,24},{40,32},{48,40},{56,48},{64,56},{72,6... | collective-permute-start | bytes 24584 | tf_op jit(solution)/shard_map/ppermute | solution.py:27
  66.0 5.5 %collective-permute-start.10 = (bf16[2,18,1,128]{3,0,2,1:T(2,128)(2,1)S(1)}, bf16[2,18,1,128]{3,0,2,1:T(2,128)(2,1)S(1)}, u32[]{:S(2)}, u32[]{:S(2)}) collective-permute-start(bf16[2,18,1,128]{3,0,2,1:T(2,128)(2,1)S(1)} %get-tuple-element.65), channel_id=1, source_target_pairs={{0,1},{1,2},{2,3},{3,4},{4,5},{5,6},{6,7},{8,9},{9,10},{10,11},{11... | collective-permute-start | bytes 27656 | tf_op jit(solution)/shard_map/ppermute | solution.py:25
  69.4 5.0 %collective-permute-start.11 = (bf16[2,18,1,128]{3,0,2,1:T(2,128)(2,1)S(1)}, bf16[2,18,1,128]{3,0,2,1:T(2,128)(2,1)S(1)}, u32[]{:S(2)}, u32[]{:S(2)}) collective-permute-start(bf16[2,18,1,128]{3,0,2,1:T(2,128)(2,1)S(1)} %get-tuple-element.66), channel_id=1, source_target_pairs={{1,0},{2,1},{3,2},{4,3},{5,4},{6,5},{7,6},{9,8},{10,9},{11,10},{12... | collective-permute-start | bytes 27656 | tf_op jit(solution)/shard_map/ppermute | solution.py:27
  79.2 16.1 %copy-start.4 = (f32[32]{0:T(128)S(1)}, f32[32]{0:T(128)}, u32[]{:S(2)}) copy-start(f32[32]{0:T(128)} %param.13) | copy-start | bytes 388
  95.4 19.5 %copy-start.2 = (bf16[3,3,3,32,32]{4,3,2,1,0:T(8,128)(2,1)S(1)}, bf16[3,3,3,32,32]{4,3,2,1,0:T(8,128)(2,1)}, u32[]{:S(2)}) copy-start(bf16[3,3,3,32,32]{4,3,2,1,0:T(8,128)(2,1)} %param.14) | copy-start | bytes 165892
  98.3 6.6 %collective-permute-start.12 = (bf16[32,1,16,128]{3,0,2,1:T(8,128)(2,1)S(1)}, bf16[32,1,16,128]{3,0,2,1:T(8,128)(2,1)S(1)}, u32[]{:S(2)}, u32[]{:S(2)}) collective-permute-start(bf16[32,1,16,128]{3,0,2,1:T(8,128)(2,1)S(1)} %get-tuple-element.32), channel_id=1, source_target_pairs={{0,8},{8,16},{16,24},{24,32},{32,40},{40,48},{48,56},{56,64},{64,7... | collective-permute-start | bytes 393224 | tf_op jit(solution)/shard_map/ppermute | solution.py:25
  102.9 6.0 %collective-permute-start.13 = (bf16[32,1,16,128]{3,0,2,1:T(8,128)(2,1)S(1)}, bf16[32,1,16,128]{3,0,2,1:T(8,128)(2,1)S(1)}, u32[]{:S(2)}, u32[]{:S(2)}) collective-permute-start(bf16[32,1,16,128]{3,0,2,1:T(8,128)(2,1)S(1)} %get-tuple-element.33), channel_id=1, source_target_pairs={{8,0},{16,8},{24,16},{32,24},{40,32},{48,40},{56,48},{64,56},{72,6... | collective-permute-start | bytes 393224 | tf_op jit(solution)/shard_map/ppermute | solution.py:27
  108.9 6.7 %collective-permute-start.14 = (bf16[32,18,1,128]{3,0,2,1:T(8,128)(2,1)S(1)}, bf16[32,18,1,128]{3,0,2,1:T(8,128)(2,1)S(1)}, u32[]{:S(2)}, u32[]{:S(2)}) collective-permute-start(bf16[32,18,1,128]{3,0,2,1:T(8,128)(2,1)S(1)} %get-tuple-element.26), channel_id=1, source_target_pairs={{0,1},{1,2},{2,3},{3,4},{4,5},{5,6},{6,7},{8,9},{9,10},{10,11},{11... | collective-permute-start | bytes 442376 | tf_op jit(solution)/shard_map/ppermute | solution.py:25
  112.9 6.5 %collective-permute-start.15 = (bf16[32,18,1,128]{3,0,2,1:T(8,128)(2,1)S(1)}, bf16[32,18,1,128]{3,0,2,1:T(8,128)(2,1)S(1)}, u32[]{:S(2)}, u32[]{:S(2)}) collective-permute-start(bf16[32,18,1,128]{3,0,2,1:T(8,128)(2,1)S(1)} %get-tuple-element.27), channel_id=1, source_target_pairs={{1,0},{2,1},{3,2},{4,3},{5,4},{6,5},{7,6},{9,8},{10,9},{11,10},{12... | collective-permute-start | bytes 442376 | tf_op jit(solution)/shard_map/ppermute | solution.py:27
  142.7 1.7 %copy-start.1 = (f32[7,16,128,32]{2,3,1,0:T(8,128)S(1)}, f32[7,16,128,32]{2,3,1,0:T(8,128)}, u32[]{:S(2)}) copy-start(f32[7,16,128,32]{2,3,1,0:T(8,128)} %fusion.53) | copy-start | bytes 5505028
  146.1 2.2 %copy-start.5 = (f32[32]{0:T(128)S(1)}, f32[32]{0:T(128)}, u32[]{:S(2)}) copy-start(f32[32]{0:T(128)} %param.15) | copy-start | bytes 388
  146.1 2.2 %copy-start.6 = (f32[2]{0:T(128)S(1)}, f32[2]{0:T(128)}, u32[]{:S(2)}) copy-start(f32[2]{0:T(128)} %param.17) | copy-start | bytes 28
where the time goes:
time: 152 us; the launch traced here: 150 us
  starting transfers between devices  44.4 us (29%)
  local copies, waits for them, and re-layouts  37.1 us (24%)
  waiting for transfers between devices  29.7 us (20%)
  matrix products  16.4 us (11%)
  other arithmetic  15.7 us (10%)
  between operations  6.4 us (4%)
    ppermute x8, starting transfers between devices, shifted(): return lax.ppermute(block, axis, route)  22.9 us
    concatenate x3, local copies, waits for them, and re-layouts, conv_rows(): stacked = jnp.concatenate(pieces, axis=0)  17.8 us
    ppermute x8, waiting for transfers between devices, shifted(): return lax.ppermute(block, axis, route)  15.9 us
    ppermute x4, starting transfers between devices, padded(): lax.ppermute(tail, axis, [(i, (i + 1) % count) for i in range(ends)])  15.1 us
    ppermute x4, waiting for transfers between devices, padded(): lax.ppermute(head, axis, [((i + 1) % count, i) for i in range(ends)])  13.1 us
    dot_general x9, matrix products, conv_rows(): jnp.einsum('ko,krcz->orcz', flat_rows[row_tap], stacked[:, row_tap:row_ta...  13 us
    unnamed x28, local copies, waits for them, and re-layouts  8.66 us
    concatenate x5, other arithmetic, padded(): jnp.concatenate([lax.ppermute(tail, axis, [(i, (i + 1) % count) for i in...  7.47 us
  transfers between devices with their start and end apart: 16, of which 8 were waited for; matrix products, arithmetic and copies ran while one was open for 2% of the time, Pallas kernels for 0%

commit v1 on v0

v1 whole, which is shorter than its diff:
```python
import jax
import jax.numpy as jnp
from jax import lax
from jax.experimental import pallas as pl
from jax.experimental.pallas import tpu as pltpu
from jax.sharding import PartitionSpec as P

MESH = pl.DeviceIdType.MESH
F32 = jnp.float32
BF16 = jnp.bfloat16
I16 = jnp.int16
STEP_Y = 4.0 / 32767
STEP_X = 12.0 / 32767
PAD = 8
CHUNKS = (32, 0, 40, 8, 16, 24)


def ramp(places, before, after):
    rise = places + 1.0 + before
    fall = 16.0 + after - places
    return jnp.clip(jnp.minimum(rise, fall), 0.0, 8.0) * 0.125


def code(values, step):
    return jnp.round(values * (1.0 / step)).astype(jnp.int32).astype(I16)


def decode(values, step):
    return values.astype(jnp.int32).astype(F32) * step


def when(condition, action):
    pl.when(condition)(action)


def iota(shape, dim):
    return lax.broadcasted_iota(jnp.int32, shape, dim).astype(F32)


def kernel(
    nx, ny,
    tiles, shifts, extents, w1, b1, w2, b2, hw, hb,
    joined, restored,
    tile, sides, landed, metas, metas_x, across, landed_x, image, stack1, first,
    w1_in, w2_in, hw_in, band1, band2, head, bias1, bias2, flat1,
    in_sem, send_y, recv_y, send_x, recv_x, send_m, recv_m, send_h, recv_h,
):
    p, q = lax.axis_index("gx"), lax.axis_index("gy")
    up, down = lax.rem(p + nx - 1, nx), lax.rem(p + 1, nx)
    left, right = lax.rem(q + ny - 1, ny), lax.rem(q + 1, ny)

    load = pltpu.make_async_copy(tiles.at[0, 0], tile.at[:, PAD:PAD + 40, PAD:PAD + 40], in_sem.at[0])
    load.start()
    loads = [
        pltpu.make_async_copy(w1, w1_in, in_sem.at[1]),
        pltpu.make_async_copy(w2, w2_in, in_sem.at[2]),
        pltpu.make_async_copy(hw, hw_in, in_sem.at[3]),
    ]
    for one in loads:
        one.start()
    barrier = pltpu.get_barrier_semaphore()
    is_up, is_down, is_left, is_right = p > 0, p < nx - 1, q > 0, q < ny - 1
    near = ((is_left, (p, left)), (is_right, (p, right)), (is_up, (up, q)), (is_down, (down, q)))
    for there_is, there in near:
        @pl.when(there_is)
        def _():
            pl.semaphore_signal(barrier, inc=1, device_id=there, device_id_type=MESH)

    @pl.when(q == 0)
    def _():
        landed[1] = jnp.zeros((2, 48, 16, 128), I16)
        metas_x[0, 1] = jnp.full((8, 128), -100.0, F32)
        image[:, :, 6:8] = jnp.zeros((2, 20, 2, 128), F32)

    @pl.when(q == ny - 1)
    def _():
        landed[0] = jnp.zeros((2, 48, 16, 128), I16)
        metas_x[0, 2] = jnp.full((8, 128), -100.0, F32)
        image[:, :, 24:26] = jnp.zeros((2, 20, 2, 128), F32)

    @pl.when(p == 0)
    def _():
        landed_x[1] = jnp.zeros((2, 16, 16, 128), I16)
        metas_x[1] = jnp.full((3, 8, 128), -100.0, F32)
        image[:, 0:2] = jnp.zeros((2, 2, 32, 128), F32)

    @pl.when(p == nx - 1)
    def _():
        landed_x[0] = jnp.zeros((2, 16, 16, 128), I16)
        metas_x[2] = jnp.full((3, 8, 128), -100.0, F32)
        image[:, 18:20] = jnp.zeros((2, 2, 32, 128), F32)

    tile[:, 0:PAD] = jnp.zeros((2, PAD, 56, 128), F32)
    tile[:, 48:56] = jnp.zeros((2, PAD, 56, 128), F32)
    tile[:, PAD:48, 0:PAD] = jnp.zeros((2, 40, PAD, 128), F32)
    tile[:, PAD:48, 48:56] = jnp.zeros((2, 40, PAD, 128), F32)

    s0, s1 = shifts[0, 0, 0], shifts[0, 0, 1]
    values = [shifts[0, 0, 0], shifts[0, 0, 1]] + [extents[0, 0, k] for k in range(4)]
    values = [v.astype(F32) for v in values]
    s0f, s1f, m0, m1, m2, m3 = values
    for k in range(6):
        metas[0, k:k + 1] = jnp.full((1, 128), values[k], F32)

    near_count = sum(there_is.astype(jnp.int32) for there_is, _ in near)
    pl.semaphore_wait(barrier, near_count)
    meta_copies = [
        pltpu.make_async_remote_copy(metas.at[0], metas_x.at[0, 2], send_m.at[0], recv_m.at[0],
                                     device_id=(p, left), device_id_type=MESH),
        pltpu.make_async_remote_copy(metas.at[0], metas_x.at[0, 1], send_m.at[1], recv_m.at[1],
                                     device_id=(p, right), device_id_type=MESH),
    ]
    when(is_left, meta_copies[0].start)
    when(is_right, meta_copies[1].start)
    load.wait()

    def own(r0, c0, width_vec):
        rows = ramp(iota((8, 1, 128), 0) + (r0 - 16.0) - s0f, m0, m1)
        weight = rows * width_vec
        return tile[:, pl.ds(r0 + 4 - s0 , 8), pl.ds(c0 + 4 - s1, 16), :] * weight[None]

    def columns(c0):
        return ramp(iota((1, 16, 128), 1) + (c0 - 16.0) - s1f, m2, m3)

    col_left, col_mid, col_right = columns(0), columns(16), columns(32)
    copies_y = []
    for k, r0 in enumerate(CHUNKS):
        for side, (c0, vec, there) in enumerate(((0, col_left, left), (32, col_right, right))):
            sides[side, :, r0:r0 + 8] = code(own(r0, c0, vec), STEP_Y)
            one = pltpu.make_async_remote_copy(
                sides.at[side, :, r0:r0 + 8], landed.at[side, :, r0:r0 + 8],
                send_y.at[side, k], recv_y.at[side, k], device_id=(p, there), device_id_type=MESH)
            when(is_right if side else is_left, one.start)
            copies_y.append(one)

    when(is_right, meta_copies[0].wait_recv)
    when(is_left, meta_copies[1].wait_recv)
    metas_x[0, 0] = metas[0]
    copies_m = [
        pltpu.make_async_remote_copy(metas_x.at[0], metas_x.at[2], send_m.at[2], recv_m.at[2],
                                     device_id=(up, q), device_id_type=MESH),
        pltpu.make_async_remote_copy(metas_x.at[0], metas_x.at[1], send_m.at[3], recv_m.at[3],
                                     device_id=(down, q), device_id_type=MESH),
    ]
    when(is_up, copies_m[0].start)
    when(is_down, copies_m[1].start)

    copies_x = []
    for k in range(4):
        r0 = CHUNKS[k]
        when(is_right, copies_y[2 * k].wait_recv)
        when(is_left, copies_y[2 * k + 1].wait_recv)
        side = 1 if r0 >= 32 else 0
        at = r0 - 32 if r0 >= 32 else r0
        total = own(r0, 16, col_mid)
        total = total + decode(landed[0, :, r0:r0 + 8], STEP_Y) + decode(landed[1, :, r0:r0 + 8], STEP_Y)
        across[side, :, at:at + 8] = code(total, STEP_X)
        one = pltpu.make_async_remote_copy(
            across.at[side, :, at:at + 8], landed_x.at[side, :, at:at + 8],
            send_x.at[k], recv_x.at[k], device_id=(down if side else up, q), device_id_type=MESH)
        when(is_down if side else is_up, one.start)
        copies_x.append(one)

    for one in loads:
        one.wait()
    bias1[...] = jnp.zeros((32, 128), F32)
    for k in range(32):
        bias1[k:k + 1] = jnp.full((1, 128), b1[k], F32)
        bias2[k:k + 1] = jnp.full((1, 128), b2[k], F32)
    flat1[...] = jnp.zeros((64, 32), F32)
    for dr in range(3):
        for dc in range(3):
            for dz in range(3):
                at = ((dz * 3 + dr) * 3 + dc) * 2
                flat1[at:at + 2] = w1_in[dr, dc, dz].astype(F32)
    tap = lax.broadcasted_iota(jnp.int32, (64, 256), 0)
    lane = lax.broadcasted_iota(jnp.int32, (64, 256), 1)
    target = (tap // 18) * 80 + ((tap // 6) % 3) * 16 + (tap % 2) * 8 + (tap // 2) % 3
    spread = jnp.where((lane == target) & (tap < 54), 1.0, 0.0).astype(BF16)
    strip = lax.dot_general(flat1[...].astype(BF16), spread, (((0,), (0,)), ((), ())),
                            preferred_element_type=F32)
    for orow in range(3):
        for ocol in range(6):
            at = (orow * 6 + ocol) * 32
            band1[at:at + 32] = pltpu.roll(strip, orow * 16 + ocol, 1).astype(BF16)
    zero = jnp.zeros((32, 128), BF16)
    for dz in range(3):
        strips = []
        for dr in range(3):
            taps = jnp.concatenate(
                [w2_in[dr, dc, dz].astype(F32) for dc in range(3)] + [jnp.zeros((32, 32), F32)], axis=0)
            taps = jnp.concatenate([taps, jnp.zeros((128, 96), F32)], axis=1)
            flipped = taps.T[0:32]
            strips.append((flipped.astype(BF16), pltpu.roll(flipped, 32, 1).astype(BF16)))
        for orow in range(2):
            for ocol in range(2):
                at = dz * 128 + (orow * 2 + ocol) * 32
                for irow in range(4):
                    dr = irow - orow
                    band2[at:at + 32, irow * 128:irow * 128 + 128] = (
                        strips[dr][ocol] if 0 <= dr < 3 else zero)
    hrow = lax.broadcasted_iota(jnp.int32, (32, 512), 0)
    hlane = lax.broadcasted_iota(jnp.int32, (32, 512), 1)
    feat = lax.broadcasted_iota(jnp.int32, (32, 512), 0)
    pick = jnp.where(feat == hlane % 32, 1.0, 0.0).astype(BF16)
    per_lane = jnp.dot(hw_in[...], pick, preferred_element_type=F32)
    cell_row = (hlane // 64) % 2
    cell_col = (hlane // 128) * 2 + (hlane // 32) % 2
    match = ((hrow // 8) % 2 == cell_row) & (hrow % 8 == cell_col)
    by_channel = jnp.where(hrow < 16, per_lane[0:1], per_lane[1:2])
    head[...] = jnp.where(match, by_channel, 0.0).astype(BF16)

    when(is_down, copies_m[0].wait_recv)
    when(is_up, copies_m[1].wait_recv)
    for k in (4, 5):
        when(is_right, copies_y[2 * k].wait_recv)
        when(is_left, copies_y[2 * k + 1].wait_recv)
    for k, one in enumerate(copies_x):
        when(is_down if CHUNKS[k] < 32 else is_up, one.wait_recv)
    for r0 in (0, 8):
        total = own(16 + r0, 16, col_mid)
        total = total + decode(landed[0, :, 16 + r0:24 + r0], STEP_Y) + decode(landed[1, :, 16 + r0:24 + r0], STEP_Y)
        total = total + decode(landed_x[0, :, r0:r0 + 8], STEP_X) + decode(landed_x[1, :, r0:r0 + 8], STEP_X)
        weights = jnp.zeros((8, 16, 128), F32)
        for i, dp in ((0, 0), (1, -1), (2, 1)):
            for j, dq in ((0, 0), (1, -1), (2, 1)):
                meta = metas_x[i, j]
                at = [meta[k:k + 1][None] for k in range(6)]
                rows = ramp(iota((8, 1, 128), 0) + (r0 - 16.0 * dp) - at[0], at[2], at[3])
                cols = ramp(iota((1, 16, 128), 1) - 16.0 * dq - at[1], at[4], at[5])
                weights = weights + rows * cols
        cells = total / weights[None]
        joined[:, r0:r0 + 8] = cells
        image[:, 2 + r0:10 + r0, 8:24] = cells

    halo = [
        (is_up, is_down, (up, q), (slice(2, 4), slice(8, 24)), (slice(18, 20), slice(8, 24))),
        (is_down, is_up, (down, q), (slice(16, 18), slice(8, 24)), (slice(0, 2), slice(8, 24))),
        (is_left, is_right, (p, left), (slice(2, 18), slice(8, 10)), (slice(2, 18), slice(24, 26))),
        (is_right, is_left, (p, right), (slice(2, 18), slice(22, 24)), (slice(2, 18), slice(6, 8))),
        (is_up & is_left, is_down & is_right, (up, left), (slice(2, 4), slice(8, 10)), (slice(18, 20), slice(24, 26))),
        (is_up & is_right, is_down & is_left, (up, right), (slice(2, 4), slice(22, 24)), (slice(18, 20), slice(6, 8))),
        (is_down & is_left, is_up & is_right, (down, left), (slice(16, 18), slice(8, 10)), (slice(0, 2), slice(24, 26))),
        (is_down & is_right, is_up & is_left, (down, right), (slice(16, 18), slice(22, 24)), (slice(0, 2), slice(6, 8))),
    ]
    copies_h = []
    for k, (out, _, there, (rs, cs), (rd, cd)) in enumerate(halo):
        one = pltpu.make_async_remote_copy(
            image.at[:, rs, cs], image.at[:, rd, cd], send_h.at[k], recv_h.at[k],
            device_id=there, device_id_type=MESH)
        when(out, one.start)
        copies_h.append(one)
    for one, way in zip(copies_h, halo):
        when(way[1], one.wait_recv)

    plane = lax.broadcasted_iota(jnp.int32, (20, 16, 128), 2)
    for cb in range(3):
        at = 6 + 6 * cb
        cells = jnp.concatenate([image[0, :, at:at + 8], image[1, :, at:at + 8]], axis=1)
        stack1[cb, 1] = cells.astype(BF16)
        stack1[cb, 0] = jnp.where(plane == 0, 0.0, pltpu.roll(cells, 1, 2)).astype(BF16)
        stack1[cb, 2] = jnp.where(plane == 127, 0.0, pltpu.roll(cells, 127, 2)).astype(BF16)

    def conv1(step, carry):
        cb, rb = step // 3, step % 3
        halves = []
        for a in range(2):
            r0 = rb * 6 + a * 3
            parts = [stack1[cb, dz, pl.ds(r0, 5)].reshape(80, 128) for dz in range(3)]
            halves.append(jnp.concatenate(parts + [jnp.zeros((16, 128), BF16)], axis=0))
        out = jnp.dot(band1[...], jnp.concatenate(halves, axis=1), preferred_element_type=F32)
        bias = jnp.concatenate([bias1[...]] * 2, axis=1)
        out = jnp.maximum(out.reshape(18, 32, 256) + bias[None], 0.0).astype(BF16)
        out = out.reshape(3, 6, 32, 256)
        for a in range(2):
            first[pl.ds(rb * 6 + a * 3, 3), pl.ds(cb * 6, 6)] = out[:, :, :, a * 128:a * 128 + 128]
        return carry

    lax.fori_loop(0, 9, conv1, 0)

    @pl.when(p == 0)
    def _():
        first[0:1] = jnp.zeros((1, 18, 32, 128), BF16)

    @pl.when(p == nx - 1)
    def _():
        first[17:18] = jnp.zeros((1, 18, 32, 128), BF16)

    @pl.when(q == 0)
    def _():
        first[:, 0:1] = jnp.zeros((18, 1, 32, 128), BF16)

    @pl.when(q == ny - 1)
    def _():
        first[:, 17:18] = jnp.zeros((18, 1, 32, 128), BF16)

    def conv2(step, carry):
        quad, half = step // 2, step % 2
        lanes = lax.broadcasted_iota(jnp.int32, (128, 256), 1) % 128
        bias = jnp.concatenate([jnp.concatenate([bias2[...]] * 4, axis=0)] * 2, axis=1)
        seconds = []
        for b in range(4):
            c0 = half * 8 + 2 * b
            blocks = [first[pl.ds(quad * 4 + 2 * a, 4), pl.ds(c0, 4)].reshape(512, 128) for a in range(2)]
            out = jnp.dot(band2[...], jnp.concatenate(blocks, axis=1), preferred_element_type=F32)
            low, high = out[0:128], out[256:384]
            low = jnp.concatenate([pltpu.roll(low[:, 0:128], 1, 1), pltpu.roll(low[:, 128:256], 1, 1)], axis=1)
            high = jnp.concatenate([pltpu.roll(high[:, 0:128], 127, 1), pltpu.roll(high[:, 128:256], 127, 1)], axis=1)
            total = out[128:256] + jnp.where(lanes == 0, 0.0, low) + jnp.where(lanes == 127, 0.0, high)
            seconds.append(jnp.maximum(total + bias, 0.0).astype(BF16))
        out = jnp.dot(head[...], jnp.concatenate(seconds, axis=0), preferred_element_type=F32)
        for ch in range(2):
            for a in range(2):
                for r in range(2):
                    at = ch * 16 + r * 8
                    restored[ch, quad * 4 + 2 * a + r, pl.ds(half * 8, 8), :] = (
                        out[at:at + 8, a * 128:a * 128 + 128] + hb[ch])
        return carry

    lax.fori_loop(0, 8, conv2, 0)

    when(is_left, meta_copies[0].wait_send)
    when(is_right, meta_copies[1].wait_send)
    for k, one in enumerate(copies_y):
        when(is_right if k % 2 else is_left, one.wait_send)
    when(is_up, copies_m[0].wait_send)
    when(is_down, copies_m[1].wait_send)
    for k, one in enumerate(copies_x):
        when(is_down if CHUNKS[k] >= 32 else is_up, one.wait_send)
    for one, way in zip(copies_h, halo):
        when(way[0], one.wait_send)


def shards(tiles, shifts, extents, w1, b1, w2, b2, hw, hb):
    nx, ny = lax.axis_size("gx"), lax.axis_size("gy")
    vmem = pl.BlockSpec(memory_space=pltpu.VMEM)
    smem = pl.BlockSpec(memory_space=pltpu.SMEM)
    hbm = pl.BlockSpec(memory_space=pl.ANY)

    def body(*refs):
        kernel(nx, ny, *refs)

    dma = pltpu.SemaphoreType.DMA
    return pl.pallas_call(
        body,
        out_shape=[jax.ShapeDtypeStruct((2, 16, 16, 128), F32)] * 2,
        in_specs=[hbm, smem, smem, hbm, smem, hbm, smem, hbm, smem],
        out_specs=[vmem, vmem],
        scratch_shapes=[
            pltpu.VMEM((2, 56, 56, 128), F32),
            pltpu.VMEM((2, 2, 48, 16, 128), I16),
            pltpu.VMEM((2, 2, 48, 16, 128), I16),
            pltpu.VMEM((1, 8, 128), F32),
            pltpu.VMEM((3, 3, 8, 128), F32),
            pltpu.VMEM((2, 2, 16, 16, 128), I16),
            pltpu.VMEM((2, 2, 16, 16, 128), I16),
            pltpu.VMEM((2, 20, 32, 128), F32),
            pltpu.VMEM((3, 3, 20, 16, 128), BF16),
            pltpu.VMEM((18, 18, 32, 128), BF16),
            pltpu.VMEM((3, 3, 3, 2, 32), BF16),
            pltpu.VMEM((3, 3, 3, 32, 32), BF16),
            pltpu.VMEM((2, 32), BF16),
            pltpu.VMEM((576, 256), BF16),
            pltpu.VMEM((384, 512), BF16),
            pltpu.VMEM((32, 512), BF16),
            pltpu.VMEM((32, 128), F32),
            pltpu.VMEM((32, 128), F32),
            pltpu.VMEM((64, 32), F32),
            dma((4,)), dma((2, 6)), dma((2, 6)), dma((4,)), dma((4,)), dma((4,)), dma((4,)), dma((8,)), dma((8,)),
        ],
        compiler_params=pltpu.CompilerParams(
            collective_id=0, has_side_effects=True, vmem_limit_bytes=60 * 1024 * 1024),
    )(tiles, shifts, extents, w1, b1, w2, b2, hw.T, hb)


def solution(mesh):
    return jax.shard_map(
        shards,
        mesh=mesh,
        in_specs=(P("gx", "gy"), P("gx", "gy"), P("gx", "gy"), P(), P(), P(), P(), P(), P()),
        out_specs=(P(None, "gx", "gy", None), P(None, "gx", "gy", None)),
        check_vma=False,
    )
```

time: 152 us -> 32.4 us (0.21)
  the two profiles are of different devices: /device:TPU:1 before, /device:TPU:97 now
where the time goes in v1:
time: 32.4 us; the launch traced here: 32.3 us
  Pallas kernels  28.3 us (87%)
  local copies, waits for them, and re-layouts  3.34 us (10%)
  between operations  0.64 us (2%)
    pallas_call x1, Pallas kernels, shards(): pl.pallas_call(body, out_shape=[jax.ShapeDtypeStruct((2, 16, 16, 128), F3...  28.3 us
    unnamed x2, local copies, waits for them, and re-layouts  3.34 us

profile of v1, /device:TPU:97, one launch (start us, length us, event | category | flops | bytes accessed | tf_op | source)
XLA Modules:
  0.0 32.3 jit_solution(6526319457532321708)
XLA Ops:
  0.6 28.3 %shard_map.104 = (f32[2,16,16,128]{3,2,1,0:T(8,128)}, f32[2,16,16,128]{3,2,1,0:T(8,128)}) custom-call(f32[1,1,2,40,40,128]{5,4,3,2,1,0:T(8,128)} %refs_0_.1, s32[1,1,2]{2,1,0:T(1,128)} %refs_1_.1, s32[1,1,4]{2,1,0:T(1,128)} %refs_2_.1, bf16[3,3,3,2,32]{4,3,2,1,0:T(2,128)(2,1)} %refs_3_.1, f32[32]{0:T(128)} %refs_4_.1, bf16[3,3,3,32,32]{4,3,2,1,0:T(8,128)(2,1)} %refs_5_.1, ...), custom_call_target="tpu_custom_call" | custom-call | tf_op jit(solution)/shard_map/pallas_call | solution.py:344
  28.9 1.7 %copy.13 = f32[2,16,16,128]{3,2,1,0:T(8,128)} copy(f32[2,16,16,128]{3,2,1,0:T(8,128)} %get-tuple-element.4) | data formatting | bytes 524288
  30.6 1.7 %copy.14 = f32[2,16,16,128]{3,2,1,0:T(8,128)} copy(f32[2,16,16,128]{3,2,1,0:T(8,128)} %get-tuple-element.5) | data formatting | bytes 524288

commit v2 on v1

--- a/solution.py
+++ b/solution.py
@@ -33,6 +33,15 @@
     pl.when(condition)(action)
 
 
+def shift_planes(x, by):
+    lane = lax.broadcasted_iota(jnp.int32, x.shape[:-1] + (128,), x.ndim - 1)
+    parts = []
+    for g in range(x.shape[-1] // 128):
+        one = pltpu.roll(x[..., g * 128:g * 128 + 128], by % 128, x.ndim - 1)
+        parts.append(jnp.where(lane == (0 if by > 0 else 127), 0.0, one))
+    return jnp.concatenate(parts, axis=-1)
+
+
 def iota(shape, dim):
     return lax.broadcasted_iota(jnp.int32, shape, dim).astype(F32)
 
@@ -42,7 +51,7 @@
     tiles, shifts, extents, w1, b1, w2, b2, hw, hb,
     joined, restored,
     tile, sides, landed, metas, metas_x, across, landed_x, image, stack1, first,
-    w1_in, w2_in, hw_in, band1, band2, head, bias1, bias2, flat1,
+    w1_in, w2_in, hw_in, band1, band2, head, bias1, bias2, flat1, second,
     in_sem, send_y, recv_y, send_x, recv_x, send_m, recv_m, send_h, recv_h,
 ):
     p, q = lax.axis_index("gx"), lax.axis_index("gy")
@@ -194,10 +203,10 @@
             strips.append((flipped.astype(BF16), pltpu.roll(flipped, 32, 1).astype(BF16)))
         for orow in range(2):
             for ocol in range(2):
-                at = dz * 128 + (orow * 2 + ocol) * 32
+                at = (orow * 2 + ocol) * 32
                 for irow in range(4):
                     dr = irow - orow
-                    band2[at:at + 32, irow * 128:irow * 128 + 128] = (
+                    band2[at:at + 32, dz * 512 + irow * 128:dz * 512 + irow * 128 + 128] = (
                         strips[dr][ocol] if 0 <= dr < 3 else zero)
     hrow = lax.broadcasted_iota(jnp.int32, (32, 512), 0)
     hlane = lax.broadcasted_iota(jnp.int32, (32, 512), 1)
@@ -253,71 +262,78 @@
     for one, way in zip(copies_h, halo):
         when(way[1], one.wait_recv)
 
-    plane = lax.broadcasted_iota(jnp.int32, (20, 16, 128), 2)
     for cb in range(3):
         at = 6 + 6 * cb
         cells = jnp.concatenate([image[0, :, at:at + 8], image[1, :, at:at + 8]], axis=1)
         stack1[cb, 1] = cells.astype(BF16)
-        stack1[cb, 0] = jnp.where(plane == 0, 0.0, pltpu.roll(cells, 1, 2)).astype(BF16)
-        stack1[cb, 2] = jnp.where(plane == 127, 0.0, pltpu.roll(cells, 127, 2)).astype(BF16)
-
-    def conv1(step, carry):
-        cb, rb = step // 3, step % 3
-        halves = []
-        for a in range(2):
-            r0 = rb * 6 + a * 3
-            parts = [stack1[cb, dz, pl.ds(r0, 5)].reshape(80, 128) for dz in range(3)]
-            halves.append(jnp.concatenate(parts + [jnp.zeros((16, 128), BF16)], axis=0))
-        out = jnp.dot(band1[...], jnp.concatenate(halves, axis=1), preferred_element_type=F32)
+        stack1[cb, 0] = shift_planes(cells, 1).astype(BF16)
+        stack1[cb, 2] = shift_planes(cells, -1).astype(BF16)
+
+    def conv1(rb, carry):
         bias = jnp.concatenate([bias1[...]] * 2, axis=1)
-        out = jnp.maximum(out.reshape(18, 32, 256) + bias[None], 0.0).astype(BF16)
-        out = out.reshape(3, 6, 32, 256)
-        for a in range(2):
-            first[pl.ds(rb * 6 + a * 3, 3), pl.ds(cb * 6, 6)] = out[:, :, :, a * 128:a * 128 + 128]
+        for cb in range(3):
+            halves = []
+            for a in range(2):
+                r0 = rb * 6 + a * 3
+                parts = [stack1[cb, dz, pl.ds(r0, 5)].reshape(80, 128) for dz in range(3)]
+                halves.append(jnp.concatenate(parts + [jnp.zeros((16, 128), BF16)], axis=0))
+            out = jnp.dot(band1[...], jnp.concatenate(halves, axis=1), preferred_element_type=F32)
+            out = jnp.maximum(out.reshape(18, 32, 256) + bias[None], 0.0)
+            for dz in range(3):
+                one = out if dz == 1 else shift_planes(out, 1 - dz)
+                one = one.astype(BF16).reshape(3, 6, 32, 256)
+                for a in range(2):
+                    first[dz, pl.ds(rb * 6 + a * 3, 3), cb * 6:cb * 6 + 6] = one[:, :, :, a * 128:a * 128 + 128]
         return carry
 
-    lax.fori_loop(0, 9, conv1, 0)
+    lax.fori_loop(0, 3, conv1, 0)
 
     @pl.when(p == 0)
     def _():
-        first[0:1] = jnp.zeros((1, 18, 32, 128), BF16)
+        first[:, 0:1] = jnp.zeros((3, 1, 18, 32, 128), BF16)
 
     @pl.when(p == nx - 1)
     def _():
-        first[17:18] = jnp.zeros((1, 18, 32, 128), BF16)
+        first[:, 17:18] = jnp.zeros((3, 1, 18, 32, 128), BF16)
 
     @pl.when(q == 0)
     def _():
-        first[:, 0:1] = jnp.zeros((18, 1, 32, 128), BF16)
+        first[:, :, 0:1] = jnp.zeros((3, 18, 1, 32, 128), BF16)
 
     @pl.when(q == ny - 1)
     def _():
-        first[:, 17:18] = jnp.zeros((18, 1, 32, 128), BF16)
-
-    def conv2(step, carry):
+        first[:, :, 17:18] = jnp.zeros((3, 18, 1, 32, 128), BF16)
+
+    bias = jnp.concatenate([jnp.concatenate([bias2[...]] * 4, axis=0)] * 4, axis=1)
+
+    def project(step):
         quad, half = step // 2, step % 2
-        lanes = lax.broadcasted_iota(jnp.int32, (128, 256), 1) % 128
-        bias = jnp.concatenate([jnp.concatenate([bias2[...]] * 4, axis=0)] * 2, axis=1)
-        seconds = []
-        for b in range(4):
-            c0 = half * 8 + 2 * b
-            blocks = [first[pl.ds(quad * 4 + 2 * a, 4), pl.ds(c0, 4)].reshape(512, 128) for a in range(2)]
-            out = jnp.dot(band2[...], jnp.concatenate(blocks, axis=1), preferred_element_type=F32)
-            low, high = out[0:128], out[256:384]
-            low = jnp.concatenate([pltpu.roll(low[:, 0:128], 1, 1), pltpu.roll(low[:, 128:256], 1, 1)], axis=1)
-            high = jnp.concatenate([pltpu.roll(high[:, 0:128], 127, 1), pltpu.roll(high[:, 128:256], 127, 1)], axis=1)
-            total = out[128:256] + jnp.where(lanes == 0, 0.0, low) + jnp.where(lanes == 127, 0.0, high)
-            seconds.append(jnp.maximum(total + bias, 0.0).astype(BF16))
-        out = jnp.dot(head[...], jnp.concatenate(seconds, axis=0), preferred_element_type=F32)
+        out = jnp.dot(head[...], second[:, step * 256:step * 256 + 256], preferred_element_type=F32)
         for ch in range(2):
             for a in range(2):
                 for r in range(2):
                     at = ch * 16 + r * 8
-                    restored[ch, quad * 4 + 2 * a + r, pl.ds(half * 8, 8), :] = (
+                    restored[ch, quad * 4 + 2 * a + r, half * 8:half * 8 + 8, :] = (
                         out[at:at + 8, a * 128:a * 128 + 128] + hb[ch])
-        return carry
-
-    lax.fori_loop(0, 8, conv2, 0)
+
+    for step in range(8):
+        quad, half = step // 2, step % 2
+        for b0 in (0, 2):
+            cols = []
+            for b in (b0, b0 + 1):
+                c0 = half * 8 + 2 * b
+                for a in range(2):
+                    r0 = quad * 4 + 2 * a
+                    cols.append(jnp.concatenate(
+                        [first[dz, r0:r0 + 4, c0:c0 + 4].reshape(512, 128) for dz in range(3)], axis=0))
+            out = jnp.dot(band2[...], jnp.concatenate(cols, axis=1), preferred_element_type=F32)
+            out = jnp.maximum(out + bias, 0.0).astype(BF16)
+            for j in range(2):
+                second[(b0 + j) * 128:(b0 + j) * 128 + 128, step * 256:step * 256 + 256] = (
+                    out[:, j * 256:j * 256 + 256])
+        if step > 0:
+            project(step - 1)
+    project(7)
 
     when(is_left, meta_copies[0].wait_send)
     when(is_right, meta_copies[1].wait_send)
@@ -343,7 +359,7 @@
     dma = pltpu.SemaphoreType.DMA
     return pl.pallas_call(
         body,
-        out_shape=[jax.ShapeDtypeStruct((2, 16, 16, 128), F32)] * 2,
+        out_shape=[pltpu.VMEM((2, 16, 16, 128), F32)] * 2,
         in_specs=[hbm, smem, smem, hbm, smem, hbm, smem, hbm, smem],
         out_specs=[vmem, vmem],
         scratch_shapes=[
@@ -356,16 +372,17 @@
             pltpu.VMEM((2, 2, 16, 16, 128), I16),
             pltpu.VMEM((2, 20, 32, 128), F32),
             pltpu.VMEM((3, 3, 20, 16, 128), BF16),
-            pltpu.VMEM((18, 18, 32, 128), BF16),
+            pltpu.VMEM((3, 18, 18, 32, 128), BF16),
             pltpu.VMEM((3, 3, 3, 2, 32), BF16),
             pltpu.VMEM((3, 3, 3, 32, 32), BF16),
             pltpu.VMEM((2, 32), BF16),
             pltpu.VMEM((576, 256), BF16),
-            pltpu.VMEM((384, 512), BF16),
+            pltpu.VMEM((128, 1536), BF16),
             pltpu.VMEM((32, 512), BF16),
             pltpu.VMEM((32, 128), F32),
             pltpu.VMEM((32, 128), F32),
             pltpu.VMEM((64, 32), F32),
+            pltpu.VMEM((512, 2048), BF16),
             dma((4,)), dma((2, 6)), dma((2, 6)), dma((4,)), dma((4,)), dma((4,)), dma((4,)), dma((8,)), dma((8,)),
         ],
         compiler_params=pltpu.CompilerParams(

time: 32.4 us -> 26.8 us (0.83)
  Pallas kernels: 28.3 us -> 24.6 us
  local copies, waits for them, and re-layouts: 3.34 us -> 1.41 us
    pallas_call x1, Pallas kernels: 28.3 us -> 24.6 us  [shards(): pl.pallas_call(body, out_shape=[pltpu.VMEM((2, 16, 16, 128), F32)] * 2, i...]
    unnamed x2, local copies, waits for them, and re-layouts: 3.34 us -> 1.41 us
where the time goes in v2:
time: 26.8 us; the launch traced here: 26.7 us
  Pallas kernels  24.6 us (92%)
  local copies, waits for them, and re-layouts  1.41 us (5%)
  between operations  0.64 us (2%)
    pallas_call x1, Pallas kernels, shards(): pl.pallas_call(body, out_shape=[pltpu.VMEM((2, 16, 16, 128), F32)] * 2, i...  24.6 us
    unnamed x2, local copies, waits for them, and re-layouts  1.41 us

profile of v2, /device:TPU:97, one launch (start us, length us, event | category | flops | bytes accessed | tf_op | source)
XLA Modules:
  0.0 26.7 jit_solution(15078749350539927326)
XLA Ops:
  0.6 24.6 %shard_map.104 = (f32[2,16,16,128]{3,2,1,0:T(8,128)S(1)}, f32[2,16,16,128]{3,2,1,0:T(8,128)S(1)}) custom-call(f32[1,1,2,40,40,128]{5,4,3,2,1,0:T(8,128)} %refs_0_.1, s32[1,1,2]{2,1,0:T(1,128)} %refs_1_.1, s32[1,1,4]{2,1,0:T(1,128)} %refs_2_.1, bf16[3,3,3,2,32]{4,3,2,1,0:T(2,128)(2,1)} %refs_3_.1, f32[32]{0:T(128)} %refs_4_.1, ...), custom_call_target="tpu_custom_call" | custom-call | tf_op jit(solution)/shard_map/pallas_call | solution.py:360
  25.3 0.7 %copy.13 = f32[2,16,16,128]{3,2,1,0:T(8,128)} copy(f32[2,16,16,128]{3,2,1,0:T(8,128)S(1)} %get-tuple-element.2) | data formatting | bytes 524288
  26.0 0.7 %copy.14 = f32[2,16,16,128]{3,2,1,0:T(8,128)} copy(f32[2,16,16,128]{3,2,1,0:T(8,128)S(1)} %get-tuple-element.3) | data formatting | bytes 524288

commit v3 on v2

v3 whole, which is shorter than its diff:
```python
import jax
import jax.numpy as jnp
from jax import lax
from jax.experimental import pallas as pl
from jax.experimental.pallas import tpu as pltpu
from jax.sharding import PartitionSpec as P

MESH = pl.DeviceIdType.MESH
F32 = jnp.float32
BF16 = jnp.bfloat16
I16 = jnp.int16
STEP_Y = 4.0 / 32767
STEP_X = 12.0 / 32767
PAD = 8
CHUNKS = ((32, 8), (0, 8), (40, 8), (8, 8), (30, 2), (16, 2), (18, 6), (24, 6))
COLUMNS = (0, 1, 4, 5, 2, 3)


def ramp(places, before, after):
    rise = places + 1.0 + before
    fall = 16.0 + after - places
    return jnp.clip(jnp.minimum(rise, fall), 0.0, 8.0) * 0.125


def code(values, step):
    return jnp.round(values * (1.0 / step)).astype(jnp.int32).astype(I16)


def decode(values, step):
    return values.astype(jnp.int32).astype(F32) * step


def when(condition, action):
    pl.when(condition)(action)


def shift_planes(x, by):
    lane = lax.broadcasted_iota(jnp.int32, x.shape[:-1] + (128,), x.ndim - 1)
    parts = []
    for g in range(x.shape[-1] // 128):
        one = pltpu.roll(x[..., g * 128:g * 128 + 128], by % 128, x.ndim - 1)
        parts.append(jnp.where(lane == (0 if by > 0 else 127), 0.0, one))
    return jnp.concatenate(parts, axis=-1)


def iota(shape, dim):
    return lax.broadcasted_iota(jnp.int32, shape, dim).astype(F32)


def kernel(
    nx, ny,
    tiles, shifts, extents, w1, b1, w2, b2, hw, hb,
    joined, restored,
    tile, sides, landed, metas, metas_x, across, landed_x, landed_far, image, stack1, first,
    w1_in, w2_in, hw_in, band1, band2, head, bias1, bias2, flat1, second, inverse,
    in_sem, send_y, recv_y, send_x, recv_x, send_m, recv_m, send_h, recv_h,
):
    p, q = lax.axis_index("gx"), lax.axis_index("gy")
    up, down = lax.rem(p + nx - 1, nx), lax.rem(p + 1, nx)
    up2, down2 = lax.rem(p + nx - 2, nx), lax.rem(p + 2, nx)
    left, right = lax.rem(q + ny - 1, ny), lax.rem(q + 1, ny)

    load = pltpu.make_async_copy(tiles.at[0, 0], tile.at[:, PAD:PAD + 40, PAD:PAD + 40], in_sem.at[0])
    load.start()
    loads = [
        pltpu.make_async_copy(w1, w1_in, in_sem.at[1]),
        pltpu.make_async_copy(w2, w2_in, in_sem.at[2]),
        pltpu.make_async_copy(hw, hw_in, in_sem.at[3]),
    ]
    for one in loads:
        one.start()
    barrier = pltpu.get_barrier_semaphore()
    is_up, is_down, is_left, is_right = p > 0, p < nx - 1, q > 0, q < ny - 1
    is_up2, is_down2 = p > 1, p < nx - 2
    near = ((is_left, (p, left)), (is_right, (p, right)), (is_up, (up, q)), (is_down, (down, q)))
    for there_is, there in near:
        @pl.when(there_is)
        def _():
            pl.semaphore_signal(barrier, inc=1, device_id=there, device_id_type=MESH)

    @pl.when(q == 0)
    def _():
        landed[1] = jnp.zeros((2, 48, 16, 128), I16)
        metas_x[2, 1] = jnp.full((8, 128), -100.0, F32)
        image[:, :, 6:8] = jnp.zeros((2, 20, 2, 128), F32)

    @pl.when(q == ny - 1)
    def _():
        landed[0] = jnp.zeros((2, 48, 16, 128), I16)
        metas_x[2, 2] = jnp.full((8, 128), -100.0, F32)
        image[:, :, 24:26] = jnp.zeros((2, 20, 2, 128), F32)

    @pl.when(p == 0)
    def _():
        landed_x[1] = jnp.zeros((2, 18, 16, 128), I16)
        metas_x[1] = jnp.full((3, 8, 128), -100.0, F32)

    @pl.when(p == nx - 1)
    def _():
        landed_x[0] = jnp.zeros((2, 18, 16, 128), I16)
        metas_x[3] = jnp.full((3, 8, 128), -100.0, F32)

    @pl.when(p <= 1)
    def _():
        landed_far[1] = jnp.zeros((2, 2, 16, 128), I16)
        metas_x[0] = jnp.full((3, 8, 128), -100.0, F32)

    @pl.when(p >= nx - 2)
    def _():
        landed_far[0] = jnp.zeros((2, 2, 16, 128), I16)
        metas_x[4] = jnp.full((3, 8, 128), -100.0, F32)

    tile[:, 0:PAD] = jnp.zeros((2, PAD, 56, 128), F32)
    tile[:, 48:56] = jnp.zeros((2, PAD, 56, 128), F32)
    tile[:, PAD:48, 0:PAD] = jnp.zeros((2, 40, PAD, 128), F32)
    tile[:, PAD:48, 48:56] = jnp.zeros((2, 40, PAD, 128), F32)

    s0, s1 = shifts[0, 0, 0], shifts[0, 0, 1]
    values = [shifts[0, 0, 0], shifts[0, 0, 1]] + [extents[0, 0, k] for k in range(4)]
    values = [v.astype(F32) for v in values]
    s0f, s1f, m0, m1, m2, m3 = values
    for k in range(6):
        metas[0, k:k + 1] = jnp.full((1, 128), values[k], F32)

    near_count = sum(there_is.astype(jnp.int32) for there_is, _ in near)
    pl.semaphore_wait(barrier, near_count)
    meta_copies = [
        pltpu.make_async_remote_copy(metas.at[0], metas_x.at[2, 2], send_m.at[0], recv_m.at[0],
                                     device_id=(p, left), device_id_type=MESH),
        pltpu.make_async_remote_copy(metas.at[0], metas_x.at[2, 1], send_m.at[1], recv_m.at[1],
                                     device_id=(p, right), device_id_type=MESH),
    ]
    when(is_left, meta_copies[0].start)
    when(is_right, meta_copies[1].start)
    load.wait()

    def own(r0, count, c0, width_vec):
        rows = ramp(iota((count, 1, 128), 0) + (r0 - 16.0) - s0f, m0, m1)
        weight = rows * width_vec
        return tile[:, pl.ds(r0 + 4 - s0 , count), pl.ds(c0 + 4 - s1, 16), :] * weight[None]

    def row_sum(r0, count):
        total = own(r0, count, 16, col_mid)
        total = total + decode(landed[0, :, r0:r0 + count], STEP_Y)
        return total + decode(landed[1, :, r0:r0 + count], STEP_Y)

    def columns(c0):
        return ramp(iota((1, 16, 128), 1) + (c0 - 16.0) - s1f, m2, m3)

    col_left, col_mid, col_right = columns(0), columns(16), columns(32)
    copies_y = []
    for k, (r0, count) in enumerate(CHUNKS):
        for side, (c0, vec, there) in enumerate(((0, col_left, left), (32, col_right, right))):
            sides[side, :, r0:r0 + count] = code(own(r0, count, c0, vec), STEP_Y)
            one = pltpu.make_async_remote_copy(
                sides.at[side, :, r0:r0 + count], landed.at[side, :, r0:r0 + count],
                send_y.at[side, k], recv_y.at[side, k], device_id=(p, there), device_id_type=MESH)
            when(is_right if side else is_left, one.start)
            copies_y.append(one)

    when(is_right, meta_copies[0].wait_recv)
    when(is_left, meta_copies[1].wait_recv)
    metas_x[2, 0] = metas[0]
    copies_m = [
        pltpu.make_async_remote_copy(metas_x.at[2], metas_x.at[2 + by], send_m.at[k], recv_m.at[k],
                                     device_id=(there, q), device_id_type=MESH)
        for k, by, there in ((2, 1, up), (3, -1, down), (4, 2, up2), (5, -2, down2))
    ]
    when(is_up, copies_m[0].start)
    when(is_down, copies_m[1].start)

    copies_x, ways_x = [], []

    def across_copy(src, dst, out, back, there):
        k = len(copies_x)
        one = pltpu.make_async_remote_copy(src, dst, send_x.at[k], recv_x.at[k],
                                           device_id=(there, q), device_id_type=MESH)
        when(out, one.start)
        copies_x.append(one)
        ways_x.append((out, back))

    for k in range(6):
        r0, count = CHUNKS[k]
        when(is_right, copies_y[2 * k].wait_recv)
        when(is_left, copies_y[2 * k + 1].wait_recv)
        side = 1 if r0 >= 30 else 0
        at = r0 - 30 * side
        across[side, :, at:at + count] = code(row_sum(r0, count), STEP_X)
        across_copy(across.at[side, :, at:at + count], landed_x.at[side, :, at:at + count],
                    is_down if side else is_up, is_up if side else is_down, down if side else up)
        if k == 3:
            when(is_down, copies_m[0].wait_recv)
            when(is_up, copies_m[1].wait_recv)
            when(is_up2, copies_m[2].start)
            when(is_down2, copies_m[3].start)
            across_copy(across.at[1, :, 16:18], landed_far.at[1], is_down2, is_up2, down2)
            across_copy(across.at[0, :, 0:2], landed_far.at[0], is_up2, is_down2, up2)

    for one in loads:
        one.wait()
    bias1[...] = jnp.zeros((32, 128), F32)
    for k in range(32):
        bias1[k:k + 1] = jnp.full((1, 128), b1[k], F32)
        bias2[k:k + 1] = jnp.full((1, 128), b2[k], F32)
    flat1[...] = jnp.zeros((64, 32), F32)
    for dr in range(3):
        for dc in range(3):
            for dz in range(3):
                at = ((dz * 3 + dr) * 3 + dc) * 2
                flat1[at:at + 2] = w1_in[dr, dc, dz].astype(F32)
    tap = lax.broadcasted_iota(jnp.int32, (64, 256), 0)
    lane = lax.broadcasted_iota(jnp.int32, (64, 256), 1)
    target = (tap // 18) * 80 + ((tap // 6) % 3) * 16 + (tap % 2) * 8 + (tap // 2) % 3
    spread = jnp.where((lane == target) & (tap < 54), 1.0, 0.0).astype(BF16)
    strip = lax.dot_general(flat1[...].astype(BF16), spread, (((0,), (0,)), ((), ())),
                            preferred_element_type=F32)
    for i, ocol in enumerate(COLUMNS):
        for orow in range(3):
            at = (i * 3 + orow) * 32
            band1[at:at + 32] = pltpu.roll(strip, orow * 16 + ocol, 1).astype(BF16)
    zero = jnp.zeros((32, 128), BF16)
    for dz in range(3):
        strips = []
        for dr in range(3):
            taps = jnp.concatenate(
                [w2_in[dr, dc, dz].astype(F32) for dc in range(3)] + [jnp.zeros((32, 32), F32)], axis=0)
            taps = jnp.concatenate([taps, jnp.zeros((128, 96), F32)], axis=1)
            flipped = taps.T[0:32]
            strips.append((flipped.astype(BF16), pltpu.roll(flipped, 32, 1).astype(BF16)))
        for orow in range(2):
            for ocol in range(2):
                at = (orow * 2 + ocol) * 32
                for irow in range(4):
                    dr = irow - orow
                    band2[at:at + 32, dz * 512 + irow * 128:dz * 512 + irow * 128 + 128] = (
                        strips[dr][ocol] if 0 <= dr < 3 else zero)
    hrow = lax.broadcasted_iota(jnp.int32, (32, 512), 0)
    hlane = lax.broadcasted_iota(jnp.int32, (32, 512), 1)
    feat = lax.broadcasted_iota(jnp.int32, (32, 512), 0)
    pick = jnp.where(feat == hlane % 32, 1.0, 0.0).astype(BF16)
    per_lane = jnp.dot(hw_in[...], pick, preferred_element_type=F32)
    cell_row = (hlane // 64) % 2
    cell_col = (hlane // 128) * 2 + (hlane // 32) % 2
    match = ((hrow // 8) % 2 == cell_row) & (hrow % 8 == cell_col)
    by_channel = jnp.where(hrow < 16, per_lane[0:1], per_lane[1:2])
    head[...] = jnp.where(match, by_channel, 0.0).astype(BF16)

    when(is_down2, copies_m[2].wait_recv)
    when(is_up2, copies_m[3].wait_recv)
    parts = ((0, 2, (-2, -1, 0)), (2, 8, (-1, 0, 1)), (10, 8, (-1, 0, 1)), (18, 2, (0, 1, 2)))
    for r0, count, reach in parts:
        weights = jnp.zeros((count, 16, 128), F32)
        for dp in reach:
            for j, dq in ((0, 0), (1, -1), (2, 1)):
                meta = metas_x[2 + dp, j]
                at = [meta[k:k + 1][None] for k in range(6)]
                rows = ramp(iota((count, 1, 128), 0) + (r0 - 2 - 16.0 * dp) - at[0], at[2], at[3])
                cols = ramp(iota((1, 16, 128), 1) - 16.0 * dq - at[1], at[4], at[5])
                weights = weights + rows * cols
        inverse[r0:r0 + count] = 1.0 / weights

    for k in (6, 7):
        when(is_right, copies_y[2 * k].wait_recv)
        when(is_left, copies_y[2 * k + 1].wait_recv)
    for one, way in zip(copies_x, ways_x):
        when(way[1], one.wait_recv)
    for r0, count, reach in parts:
        total = row_sum(14 + r0, count)
        if r0 < 18:
            total = total + decode(landed_x[1, :, r0:r0 + count], STEP_X)
        else:
            total = total + decode(landed_far[0], STEP_X)
        if r0 >= 2:
            total = total + decode(landed_x[0, :, r0 - 2:r0 - 2 + count], STEP_X)
        else:
            total = total + decode(landed_far[1], STEP_X)
        cells = total * inverse[r0:r0 + count][None]
        image[:, r0:r0 + count, 8:24] = cells
        if count == 8:
            joined[:, r0 - 2:r0 + 6] = cells

    @pl.when(p == 0)
    def _():
        image[:, 0:2, 8:24] = jnp.zeros((2, 2, 16, 128), F32)

    @pl.when(p == nx - 1)
    def _():
        image[:, 18:20, 8:24] = jnp.zeros((2, 2, 16, 128), F32)

    copies_h = [
        pltpu.make_async_remote_copy(
            image.at[:, :, src:src + 2], image.at[:, :, dst:dst + 2], send_h.at[k], recv_h.at[k],
            device_id=(p, there), device_id_type=MESH)
        for k, src, dst, there in ((0, 8, 24, left), (1, 22, 6, right))
    ]
    when(is_left, copies_h[0].start)
    when(is_right, copies_h[1].start)

    def stack(block, cells):
        stack1[block, 1] = cells.astype(BF16)
        stack1[block, 0] = shift_planes(cells, 1).astype(BF16)
        stack1[block, 2] = shift_planes(cells, -1).astype(BF16)

    def conv1(block, rows, low, high, places):
        halves = []
        for r0 in rows:
            parts = [stack1[block, dz, pl.ds(r0, 5)].reshape(80, 128) for dz in range(3)]
            halves.append(jnp.concatenate(parts + [jnp.zeros((16, 128), BF16)], axis=0))
        count, lanes = (high - low) // 96, 128 * len(rows)
        bias = jnp.concatenate([bias1[...]] * len(rows), axis=1)
        out = jnp.dot(band1[low:high], jnp.concatenate(halves, axis=1), preferred_element_type=F32)
        out = jnp.maximum(out.reshape(3 * count, 32, lanes) + bias[None], 0.0)
        for dz in range(3):
            one = out if dz == 1 else shift_planes(out, 1 - dz)
            one = one.astype(BF16).reshape(count, 3, 32, lanes)
            for a, r0 in enumerate(rows):
                for i, place in enumerate(places):
                    first[dz, pl.ds(r0, 3), place] = one[i, :, :, a * 128:a * 128 + 128]

    for block, at in ((0, 8), (1, 14), (2, 16)):
        stack(block, jnp.concatenate([image[0, :, at:at + 8], image[1, :, at:at + 8]], axis=1))

    def inner(i, carry):
        rows = (i * 6, i * 6 + 3)
        conv1(0, rows, 0, 576, [2 + c for c in COLUMNS])
        conv1(1, rows, 0, 576, [8 + c for c in COLUMNS])
        conv1(2, rows, 192, 384, [14, 15])
        return carry

    lax.fori_loop(0, 3, inner, 0)

    def clear_rows(low, high):
        @pl.when(p == 0)
        def _():
            first[:, 0:1, low:high] = jnp.zeros((3, 1, high - low, 32, 128), BF16)

        @pl.when(p == nx - 1)
        def _():
            first[:, 17:18, low:high] = jnp.zeros((3, 1, high - low, 32, 128), BF16)

    clear_rows(2, 16)

    bias = jnp.concatenate([jnp.concatenate([bias2[...]] * 4, axis=0)] * 4, axis=1)

    def conv2(quad, blocks, slot, b0):
        cols = []
        for c0 in blocks:
            for a in range(2):
                r0 = quad * 4 + 2 * a
                cols.append(jnp.concatenate(
                    [first[dz, r0:r0 + 4, c0:c0 + 4].reshape(512, 128) for dz in range(3)], axis=0))
        out = jnp.dot(band2[...], jnp.concatenate(cols, axis=1), preferred_element_type=F32)
        out = jnp.maximum(out + bias, 0.0).astype(BF16)
        for j in range(2):
            second[(b0 + j) * 128:(b0 + j) * 128 + 128, slot * 256:slot * 256 + 256] = (
                out[:, j * 256:j * 256 + 256])

    def project(quad, slot, places):
        out = jnp.dot(head[...], second[:, slot * 256:slot * 256 + 256], preferred_element_type=F32)
        for ch in range(2):
            for a in range(2):
                for r in range(2):
                    cells = out[ch * 16 + r * 8:ch * 16 + r * 8 + 8, a * 128:a * 128 + 128] + hb[ch]
                    for src, dst, count in places:
                        restored[ch, quad * 4 + 2 * a + r, dst:dst + count, :] = cells[src:src + count]

    for quad in range(4):
        conv2(quad, (2, 4), quad, 0)
        conv2(quad, (6, 8), quad, 2)
        conv2(quad, (10, 12), 4 + quad, 0)
        if quad > 0:
            project(quad - 1, quad - 1, ((0, 2, 8),))

    when(is_right, copies_h[0].wait_recv)
    when(is_left, copies_h[1].wait_recv)
    stack(3, jnp.concatenate(
        [image[0, :, 6:10], image[0, :, 22:26], image[1, :, 6:10], image[1, :, 22:26]], axis=1))
    conv1(3, (0, 3, 6, 9, 12, 15), 0, 384, [0, 1, 16, 17])
    clear_rows(0, 18)

    @pl.when(q == 0)
    def _():
        first[:, :, 0:1] = jnp.zeros((3, 18, 1, 32, 128), BF16)

    @pl.when(q == ny - 1)
    def _():
        first[:, :, 17:18] = jnp.zeros((3, 18, 1, 32, 128), BF16)

    project(3, 3, ((0, 2, 8),))
    for quad in range(4):
        conv2(quad, (0, 14), 4 + quad, 2)
        if quad > 0:
            project(quad - 1, 3 + quad, ((0, 10, 4), (4, 0, 2), (6, 14, 2)))
    project(3, 7, ((0, 10, 4), (4, 0, 2), (6, 14, 2)))

    when(is_left, meta_copies[0].wait_send)
    when(is_right, meta_copies[1].wait_send)
    for k, one in enumerate(copies_y):
        when(is_right if k % 2 else is_left, one.wait_send)
    for one, way in zip(copies_m, (is_up, is_down, is_up2, is_down2)):
        when(way, one.wait_send)
    for one, way in zip(copies_x, ways_x):
        when(way[0], one.wait_send)
    when(is_left, copies_h[0].wait_send)
    when(is_right, copies_h[1].wait_send)


def shards(tiles, shifts, extents, w1, b1, w2, b2, hw, hb):
    nx, ny = lax.axis_size("gx"), lax.axis_size("gy")
    vmem = pl.BlockSpec(memory_space=pltpu.VMEM)
    smem = pl.BlockSpec(memory_space=pltpu.SMEM)
    hbm = pl.BlockSpec(memory_space=pl.ANY)

    def body(*refs):
        kernel(nx, ny, *refs)

    dma = pltpu.SemaphoreType.DMA
    return pl.pallas_call(
        body,
        out_shape=[pltpu.VMEM((2, 16, 16, 128), F32)] * 2,
        in_specs=[hbm, smem, smem, hbm, smem, hbm, smem, hbm, smem],
        out_specs=[vmem, vmem],
        scratch_shapes=[
            pltpu.VMEM((2, 56, 56, 128), F32),
            pltpu.VMEM((2, 2, 48, 16, 128), I16),
            pltpu.VMEM((2, 2, 48, 16, 128), I16),
            pltpu.VMEM((1, 8, 128), F32),
            pltpu.VMEM((5, 3, 8, 128), F32),
            pltpu.VMEM((2, 2, 18, 16, 128), I16),
            pltpu.VMEM((2, 2, 18, 16, 128), I16),
            pltpu.VMEM((2, 2, 2, 16, 128), I16),
            pltpu.VMEM((2, 20, 32, 128), F32),
            pltpu.VMEM((4, 3, 20, 16, 128), BF16),
            pltpu.VMEM((3, 18, 18, 32, 128), BF16),
            pltpu.VMEM((3, 3, 3, 2, 32), BF16),
            pltpu.VMEM((3, 3, 3, 32, 32), BF16),
            pltpu.VMEM((2, 32), BF16),
            pltpu.VMEM((576, 256), BF16),
            pltpu.VMEM((128, 1536), BF16),
            pltpu.VMEM((32, 512), BF16),
            pltpu.VMEM((32, 128), F32),
            pltpu.VMEM((32, 128), F32),
            pltpu.VMEM((64, 32), F32),
            pltpu.VMEM((512, 2048), BF16),
            pltpu.VMEM((20, 16, 128), F32),
            dma((4,)), dma((2, 8)), dma((2, 8)), dma((8,)), dma((8,)), dma((6,)), dma((6,)), dma((2,)), dma((2,)),
        ],
        compiler_params=pltpu.CompilerParams(
            collective_id=0, has_side_effects=True, vmem_limit_bytes=60 * 1024 * 1024),
    )(tiles, shifts, extents, w1, b1, w2, b2, hw.T, hb)


def solution(mesh):
    return jax.shard_map(
        shards,
        mesh=mesh,
        in_specs=(P("gx", "gy"), P("gx", "gy"), P("gx", "gy"), P(), P(), P(), P(), P(), P()),
        out_specs=(P(None, "gx", "gy", None), P(None, "gx", "gy", None)),
        check_vma=False,
    )
```

time: 26.8 us -> 23.8 us (0.89)
  the two profiles are of different devices: /device:TPU:97 before, /device:TPU:1 now
where the time goes in v3:
time: 23.8 us; the launch traced here: 23.5 us
  Pallas kernels  21.4 us (90%)
  local copies, waits for them, and re-layouts  1.41 us (6%)
  between operations  0.64 us (3%)
    pallas_call x1, Pallas kernels, shards(): pl.pallas_call(body, out_shape=[pltpu.VMEM((2, 16, 16, 128), F32)] * 2, i...  21.4 us
    unnamed x2, local copies, waits for them, and re-layouts  1.41 us

profile of v3, /device:TPU:1, one launch (start us, length us, event | category | flops | bytes accessed | tf_op | source)
XLA Modules:
  0.0 23.5 jit_solution(12313213942773288129)
XLA Ops:
  0.6 21.4 %shard_map.104 = (f32[2,16,16,128]{3,2,1,0:T(8,128)S(1)}, f32[2,16,16,128]{3,2,1,0:T(8,128)S(1)}) custom-call(f32[1,1,2,40,40,128]{5,4,3,2,1,0:T(8,128)} %refs_0_.1, s32[1,1,2]{2,1,0:T(1,128)} %refs_1_.1, s32[1,1,4]{2,1,0:T(1,128)} %refs_2_.1, bf16[3,3,3,2,32]{4,3,2,1,0:T(2,128)(2,1)} %refs_3_.1, f32[32]{0:T(128)} %refs_4_.1, ...), custom_call_target="tpu_custom_call" | custom-call | tf_op jit(solution)/shard_map/pallas_call | solution.py:418
  22.1 0.7 %copy.13 = f32[2,16,16,128]{3,2,1,0:T(8,128)} copy(f32[2,16,16,128]{3,2,1,0:T(8,128)S(1)} %get-tuple-element.2) | data formatting | bytes 524288
  22.8 0.7 %copy.14 = f32[2,16,16,128]{3,2,1,0:T(8,128)} copy(f32[2,16,16,128]{3,2,1,0:T(8,128)S(1)} %get-tuple-element.3) | data formatting | bytes 524288

commit v4 on v3

--- a/solution.py
+++ b/solution.py
@@ -13,6 +13,8 @@
 STEP_X = 12.0 / 32767
 PAD = 8
 CHUNKS = ((32, 8), (0, 8), (40, 8), (8, 8), (30, 2), (16, 2), (18, 6), (24, 6))
+FOLDED = 6
+MAIN = 4
 COLUMNS = (0, 1, 4, 5, 2, 3)
 
 
@@ -23,7 +25,7 @@
 
 
 def code(values, step):
-    return jnp.round(values * (1.0 / step)).astype(jnp.int32).astype(I16)
+    return (values * (1.0 / step) + 0.5).astype(jnp.int32).astype(I16)
 
 
 def decode(values, step):
@@ -39,7 +41,7 @@
     parts = []
     for g in range(x.shape[-1] // 128):
         one = pltpu.roll(x[..., g * 128:g * 128 + 128], by % 128, x.ndim - 1)
-        parts.append(jnp.where(lane == (0 if by > 0 else 127), 0.0, one))
+        parts.append(jnp.where(lane == (0 if by > 0 else 127), jnp.zeros_like(one), one))
     return jnp.concatenate(parts, axis=-1)
 
 
@@ -49,10 +51,10 @@
 
 def kernel(
     nx, ny,
-    tiles, shifts, extents, w1, b1, w2, b2, hw, hb,
+    tiles, shifts_in, extents_in, w1, b1_in, w2, b2_in, hw, hb_in,
     joined, restored,
     tile, sides, landed, metas, metas_x, across, landed_x, landed_far, image, stack1, first,
-    w1_in, w2_in, hw_in, band1, band2, head, bias1, bias2, flat1, second, inverse,
+    w1_in, w2_in, hw_in, band1, band2, head, bias1, bias2, flat1, second, inverse, shifts, extents, b1, b2, hb, small_sem,
     in_sem, send_y, recv_y, send_x, recv_x, send_m, recv_m, send_h, recv_h,
 ):
     p, q = lax.axis_index("gx"), lax.axis_index("gy")
@@ -60,6 +62,22 @@
     up2, down2 = lax.rem(p + nx - 2, nx), lax.rem(p + 2, nx)
     left, right = lax.rem(q + ny - 1, ny), lax.rem(q + 1, ny)
 
+    barrier = pltpu.get_barrier_semaphore()
+    is_up, is_down, is_left, is_right = p > 0, p < nx - 1, q > 0, q < ny - 1
+    is_up2, is_down2 = p > 1, p < nx - 2
+    near = ((is_left, (p, left)), (is_right, (p, right)), (is_up, (up, q)), (is_down, (down, q)))
+    for there_is, there in near:
+        @pl.when(there_is)
+        def _():
+            pl.semaphore_signal(barrier, inc=1, device_id=there, device_id_type=MESH)
+
+    small = [
+        pltpu.make_async_copy(src, dst, small_sem.at[k])
+        for k, (src, dst) in enumerate(
+            ((shifts_in, shifts), (extents_in, extents), (b1_in, b1), (b2_in, b2), (hb_in, hb)))
+    ]
+    for one in small:
+        one.start()
     load = pltpu.make_async_copy(tiles.at[0, 0], tile.at[:, PAD:PAD + 40, PAD:PAD + 40], in_sem.at[0])
     load.start()
     loads = [
@@ -69,15 +87,6 @@
     ]
     for one in loads:
         one.start()
-    barrier = pltpu.get_barrier_semaphore()
-    is_up, is_down, is_left, is_right = p > 0, p < nx - 1, q > 0, q < ny - 1
-    is_up2, is_down2 = p > 1, p < nx - 2
-    near = ((is_left, (p, left)), (is_right, (p, right)), (is_up, (up, q)), (is_down, (down, q)))
-    for there_is, there in near:
-        @pl.when(there_is)
-        def _():
-            pl.semaphore_signal(barrier, inc=1, device_id=there, device_id_type=MESH)
-
     @pl.when(q == 0)
     def _():
         landed[1] = jnp.zeros((2, 48, 16, 128), I16)
@@ -115,6 +124,8 @@
     tile[:, PAD:48, 0:PAD] = jnp.zeros((2, 40, PAD, 128), F32)
     tile[:, PAD:48, 48:56] = jnp.zeros((2, 40, PAD, 128), F32)
 
+    small[0].wait()
+    small[1].wait()
     s0, s1 = shifts[0, 0, 0], shifts[0, 0, 1]
     values = [shifts[0, 0, 0], shifts[0, 0, 1]] + [extents[0, 0, k] for k in range(4)]
     values = [v.astype(F32) for v in values]
@@ -179,7 +190,7 @@
         copies_x.append(one)
         ways_x.append((out, back))
 
-    for k in range(6):
+    for k in range(FOLDED):
         r0, count = CHUNKS[k]
         when(is_right, copies_y[2 * k].wait_recv)
         when(is_left, copies_y[2 * k + 1].wait_recv)
@@ -188,7 +199,7 @@
         across[side, :, at:at + count] = code(row_sum(r0, count), STEP_X)
         across_copy(across.at[side, :, at:at + count], landed_x.at[side, :, at:at + count],
                     is_down if side else is_up, is_up if side else is_down, down if side else up)
-        if k == 3:
+        if k == MAIN - 1:
             when(is_down, copies_m[0].wait_recv)
             when(is_up, copies_m[1].wait_recv)
             when(is_up2, copies_m[2].start)
@@ -198,7 +209,8 @@
 
     for one in loads:
         one.wait()
-    bias1[...] = jnp.zeros((32, 128), F32)
+    for one in small[2:]:
+        one.wait()
     for k in range(32):
         bias1[k:k + 1] = jnp.full((1, 128), b1[k], F32)
         bias2[k:k + 1] = jnp.full((1, 128), b2[k], F32)
@@ -259,13 +271,14 @@
                 weights = weights + rows * cols
         inverse[r0:r0 + count] = 1.0 / weights
 
-    for k in (6, 7):
+    for k in range(FOLDED, len(CHUNKS)):
         when(is_right, copies_y[2 * k].wait_recv)
         when(is_left, copies_y[2 * k + 1].wait_recv)
-    for one, way in zip(copies_x, ways_x):
-        when(way[1], one.wait_recv)
-    for r0, count, reach in parts:
-        total = row_sum(14 + r0, count)
+    for r0, count, _ in parts:
+        image[:, r0:r0 + count, 8:24] = row_sum(14 + r0, count)
+
+    def fold(r0, count):
+        total = image[:, r0:r0 + count, 8:24]
         if r0 < 18:
             total = total + decode(landed_x[1, :, r0:r0 + count], STEP_X)
         else:
@@ -276,58 +289,76 @@
             total = total + decode(landed_far[1], STEP_X)
         cells = total * inverse[r0:r0 + count][None]
         image[:, r0:r0 + count, 8:24] = cells
-        if count == 8:
-            joined[:, r0 - 2:r0 + 6] = cells
-
-    @pl.when(p == 0)
-    def _():
-        image[:, 0:2, 8:24] = jnp.zeros((2, 2, 16, 128), F32)
-
-    @pl.when(p == nx - 1)
-    def _():
-        image[:, 18:20, 8:24] = jnp.zeros((2, 2, 16, 128), F32)
+        return cells
 
     copies_h = [
         pltpu.make_async_remote_copy(
-            image.at[:, :, src:src + 2], image.at[:, :, dst:dst + 2], send_h.at[k], recv_h.at[k],
+            image.at[:, r0:r0 + count, src:src + 2], image.at[:, r0:r0 + count, dst:dst + 2],
+            send_h.at[2 * k + way], recv_h.at[2 * k + way],
             device_id=(p, there), device_id_type=MESH)
-        for k, src, dst, there in ((0, 8, 24, left), (1, 22, 6, right))
+        for k, (r0, count) in enumerate(((2, 16), (0, 2), (18, 2)))
+        for way, src, dst, there in ((0, 8, 24, left), (1, 22, 6, right))
     ]
+    for k in range(MAIN):
+        when(ways_x[k][1], copies_x[k].wait_recv)
+    for r0 in (2, 10):
+        joined[:, r0 - 2:r0 + 6] = fold(r0, 8)
     when(is_left, copies_h[0].start)
     when(is_right, copies_h[1].start)
 
-    def stack(block, cells):
-        stack1[block, 1] = cells.astype(BF16)
-        stack1[block, 0] = shift_planes(cells, 1).astype(BF16)
-        stack1[block, 2] = shift_planes(cells, -1).astype(BF16)
+    def stack(block, at, rows):
+        cells = jnp.concatenate([image[ch, rows, c:c + 8 // len(at)] for ch in range(2) for c in at], axis=1)
+        stack1[block, 1, rows] = cells.astype(BF16)
+        stack1[block, 0, rows] = shift_planes(cells, 1).astype(BF16)
+        stack1[block, 2, rows] = shift_planes(cells, -1).astype(BF16)
 
     def conv1(block, rows, low, high, places):
         halves = []
         for r0 in rows:
-            parts = [stack1[block, dz, pl.ds(r0, 5)].reshape(80, 128) for dz in range(3)]
+            parts = [stack1[block, dz, r0:r0 + 5].reshape(80, 128) for dz in range(3)]
             halves.append(jnp.concatenate(parts + [jnp.zeros((16, 128), BF16)], axis=0))
         count, lanes = (high - low) // 96, 128 * len(rows)
         bias = jnp.concatenate([bias1[...]] * len(rows), axis=1)
         out = jnp.dot(band1[low:high], jnp.concatenate(halves, axis=1), preferred_element_type=F32)
-        out = jnp.maximum(out.reshape(3 * count, 32, lanes) + bias[None], 0.0)
+        out = jnp.maximum(out.reshape(3 * count, 32, lanes) + bias[None], 0.0).astype(BF16)
         for dz in range(3):
             one = out if dz == 1 else shift_planes(out, 1 - dz)
-            one = one.astype(BF16).reshape(count, 3, 32, lanes)
+            one = one.reshape(count, 3, 32, lanes)
             for a, r0 in enumerate(rows):
                 for i, place in enumerate(places):
-                    first[dz, pl.ds(r0, 3), place] = one[i, :, :, a * 128:a * 128 + 128]
-
-    for block, at in ((0, 8), (1, 14), (2, 16)):
-        stack(block, jnp.concatenate([image[0, :, at:at + 8], image[1, :, at:at + 8]], axis=1))
-
-    def inner(i, carry):
-        rows = (i * 6, i * 6 + 3)
+                    first[dz, r0:r0 + 3, place] = one[i, :, :, a * 128:a * 128 + 128]
+
+    def inner(rows):
         conv1(0, rows, 0, 576, [2 + c for c in COLUMNS])
         conv1(1, rows, 0, 576, [8 + c for c in COLUMNS])
         conv1(2, rows, 192, 384, [14, 15])
-        return carry
-
-    lax.fori_loop(0, 3, inner, 0)
+
+    blocks = ((0, (8,)), (1, (14,)), (2, (16,)))
+    for block, at in blocks:
+        stack(block, at, slice(2, 18))
+    inner((3, 6))
+    inner((9, 12))
+
+    for one, way in zip(copies_x[MAIN:], ways_x[MAIN:]):
+        when(way[1], one.wait_recv)
+    fold(0, 2)
+    fold(18, 2)
+
+    @pl.when(p == 0)
+    def _():
+        image[:, 0:2, 8:24] = jnp.zeros((2, 2, 16, 128), F32)
+
+    @pl.when(p == nx - 1)
+    def _():
+        image[:, 18:20, 8:24] = jnp.zeros((2, 2, 16, 128), F32)
+
+    for k in (1, 2):
+        when(is_left, copies_h[2 * k].start)
+        when(is_right, copies_h[2 * k + 1].start)
+    for block, at in blocks:
+        stack(block, at, slice(0, 2))
+        stack(block, at, slice(18, 20))
+    inner((0, 15))
 
     def clear_rows(low, high):
         @pl.when(p == 0)
@@ -371,10 +402,10 @@
         if quad > 0:
             project(quad - 1, quad - 1, ((0, 2, 8),))
 
-    when(is_right, copies_h[0].wait_recv)
-    when(is_left, copies_h[1].wait_recv)
-    stack(3, jnp.concatenate(
-        [image[0, :, 6:10], image[0, :, 22:26], image[1, :, 6:10], image[1, :, 22:26]], axis=1))
+    for k in range(3):
+        when(is_right, copies_h[2 * k].wait_recv)
+        when(is_left, copies_h[2 * k + 1].wait_recv)
+    stack(3, (6, 22), slice(0, 20))
     conv1(3, (0, 3, 6, 9, 12, 15), 0, 384, [0, 1, 16, 17])
     clear_rows(0, 18)
 
@@ -401,24 +432,24 @@
         when(way, one.wait_send)
     for one, way in zip(copies_x, ways_x):
         when(way[0], one.wait_send)
-    when(is_left, copies_h[0].wait_send)
-    when(is_right, copies_h[1].wait_send)
+    for k in range(3):
+        when(is_left, copies_h[2 * k].wait_send)
+        when(is_right, copies_h[2 * k + 1].wait_send)
 
 
 def shards(tiles, shifts, extents, w1, b1, w2, b2, hw, hb):
     nx, ny = lax.axis_size("gx"), lax.axis_size("gy")
     vmem = pl.BlockSpec(memory_space=pltpu.VMEM)
-    smem = pl.BlockSpec(memory_space=pltpu.SMEM)
     hbm = pl.BlockSpec(memory_space=pl.ANY)
 
     def body(*refs):
         kernel(nx, ny, *refs)
 
     dma = pltpu.SemaphoreType.DMA
-    return pl.pallas_call(
+    made = pl.pallas_call(
         body,
         out_shape=[pltpu.VMEM((2, 16, 16, 128), F32)] * 2,
-        in_specs=[hbm, smem, smem, hbm, smem, hbm, smem, hbm, smem],
+        in_specs=[hbm] * 9,
         out_specs=[vmem, vmem],
         scratch_shapes=[
             pltpu.VMEM((2, 56, 56, 128), F32),
@@ -443,11 +474,36 @@
             pltpu.VMEM((64, 32), F32),
             pltpu.VMEM((512, 2048), BF16),
             pltpu.VMEM((20, 16, 128), F32),
-            dma((4,)), dma((2, 8)), dma((2, 8)), dma((8,)), dma((8,)), dma((6,)), dma((6,)), dma((2,)), dma((2,)),
+            pltpu.SMEM((1, 1, 2), jnp.int32),
+            pltpu.SMEM((1, 1, 4), jnp.int32),
+            pltpu.SMEM((32,), F32),
+            pltpu.SMEM((32,), F32),
+            pltpu.SMEM((2,), F32),
+            dma((5,)),
+            dma((4,)), dma((2, len(CHUNKS))), dma((2, len(CHUNKS))), dma((FOLDED + 2,)), dma((FOLDED + 2,)), dma((6,)), dma((6,)), dma((6,)), dma((6,)),
         ],
         compiler_params=pltpu.CompilerParams(
             collective_id=0, has_side_effects=True, vmem_limit_bytes=60 * 1024 * 1024),
     )(tiles, shifts, extents, w1, b1, w2, b2, hw.T, hb)
+    return pl.pallas_call(
+        hand_over,
+        out_shape=[jax.ShapeDtypeStruct((2, 16, 16, 128), F32)] * 2,
+        in_specs=[vmem, vmem],
+        out_specs=[hbm, hbm],
+        scratch_shapes=[dma((4,))],
+        compiler_params=pltpu.CompilerParams(vmem_limit_bytes=16 * 1024 * 1024),
+    )(*made)
+
+
+def hand_over(joined, restored, joined_out, restored_out, sem):
+    copies = []
+    for k, (src, dst) in enumerate(((joined, joined_out), (restored, restored_out))):
+        for ch in range(2):
+            one = pltpu.make_async_copy(src.at[ch], dst.at[ch], sem.at[2 * k + ch])
+            one.start()
+            copies.append(one)
+    for one in copies:
+        one.wait()
 
 
 def solution(mesh):

time: 23.8 us -> 22.4 us (0.941)
  local copies, waits for them, and re-layouts: 1.41 us -> 0 us
    unnamed x2 -> x0, local copies, waits for them, and re-layouts: 1.41 us -> none
    pallas_call x0 -> x1, Pallas kernels: none -> 0.82 us  [shards(): pl.pallas_call(hand_over, out_shape=[jax.ShapeDtypeStruct((2, 16, 16, 128...]
    pallas_call x1, Pallas kernels: 21.4 us -> 20.6 us  [shards(): pl.pallas_call(body, out_shape=[pltpu.VMEM((2, 16, 16, 128), F32)] * 2, i...]
where the time goes in v4:
time: 22.4 us; the launch traced here: 22.1 us
  Pallas kernels  21.5 us (96%)
  between operations  0.64 us (3%)
    pallas_call x1, Pallas kernels, shards(): pl.pallas_call(body, out_shape=[pltpu.VMEM((2, 16, 16, 128), F32)] * 2, i...  20.6 us
    pallas_call x1, Pallas kernels, shards(): pl.pallas_call(hand_over, out_shape=[jax.ShapeDtypeStruct((2, 16, 16, 128...  0.82 us

profile of v4, /device:TPU:1, one launch (start us, length us, event | category | flops | bytes accessed | tf_op | source)
XLA Modules:
  0.0 22.1 jit_solution(12308947907818297507)
XLA Ops:
  0.6 20.6 %shard_map.104 = (f32[2,16,16,128]{3,2,1,0:T(8,128)S(1)}, f32[2,16,16,128]{3,2,1,0:T(8,128)S(1)}) custom-call(f32[1,1,2,40,40,128]{5,4,3,2,1,0:T(8,128)} %refs_0_.1, s32[1,1,2]{2,1,0:T(1,128)} %refs_1_.1, s32[1,1,4]{2,1,0:T(1,128)} %refs_2_.1, bf16[3,3,3,2,32]{4,3,2,1,0:T(2,128)(2,1)} %refs_3_.1, f32[32]{0:T(128)} %refs_4_.1, ...), custom_call_target="tpu_custom_call" | custom-call | tf_op jit(solution)/shard_map/pallas_call | solution.py:449
  21.3 0.8 %shard_map.105 = (f32[2,16,16,128]{3,2,1,0:T(8,128)}, f32[2,16,16,128]{3,2,1,0:T(8,128)}) custom-call(f32[2,16,16,128]{3,2,1,0:T(8,128)S(1)} %get-tuple-element.4.joined, f32[2,16,16,128]{3,2,1,0:T(8,128)S(1)} %get-tuple-element.5.restored), custom_call_target="tpu_custom_call" | custom-call | tf_op jit(solution)/shard_map/pallas_call | solution.py:488

commit v5 on v4

--- a/solution.py
+++ b/solution.py
@@ -12,9 +12,9 @@
 STEP_Y = 4.0 / 32767
 STEP_X = 12.0 / 32767
 PAD = 8
-CHUNKS = ((32, 8), (0, 8), (40, 8), (8, 8), (30, 2), (16, 2), (18, 6), (24, 6))
-FOLDED = 6
-MAIN = 4
+CHUNKS = ((32, 4), (0, 4), (36, 4), (4, 4), (40, 8), (8, 8), (30, 2), (16, 2), (18, 6), (24, 6))
+FOLDED = 8
+MAIN = 6
 COLUMNS = (0, 1, 4, 5, 2, 3)
 
 

time: 22.4 us -> 22.4 us (level)
  no operation moved by 1% of the time
where the time goes in v5:
time: 22.4 us; the launch traced here: 22.2 us
  Pallas kernels  21.6 us (96%)
  between operations  0.64 us (3%)
    pallas_call x1, Pallas kernels, shards(): pl.pallas_call(body, out_shape=[pltpu.VMEM((2, 16, 16, 128), F32)] * 2, i...  20.8 us
    pallas_call x1, Pallas kernels, shards(): pl.pallas_call(hand_over, out_shape=[jax.ShapeDtypeStruct((2, 16, 16, 128...  0.82 us

profile of v5, /device:TPU:1, one launch (start us, length us, event | category | flops | bytes accessed | tf_op | source)
XLA Modules:
  0.0 22.2 jit_solution(10964097018663325030)
XLA Ops:
  0.6 20.8 %shard_map.104 = (f32[2,16,16,128]{3,2,1,0:T(8,128)S(1)}, f32[2,16,16,128]{3,2,1,0:T(8,128)S(1)}) custom-call(f32[1,1,2,40,40,128]{5,4,3,2,1,0:T(8,128)} %refs_0_.1, s32[1,1,2]{2,1,0:T(1,128)} %refs_1_.1, s32[1,1,4]{2,1,0:T(1,128)} %refs_2_.1, bf16[3,3,3,2,32]{4,3,2,1,0:T(2,128)(2,1)} %refs_3_.1, f32[32]{0:T(128)} %refs_4_.1, ...), custom_call_target="tpu_custom_call" | custom-call | tf_op jit(solution)/shard_map/pallas_call | solution.py:449
  21.4 0.8 %shard_map.105 = (f32[2,16,16,128]{3,2,1,0:T(8,128)}, f32[2,16,16,128]{3,2,1,0:T(8,128)}) custom-call(f32[2,16,16,128]{3,2,1,0:T(8,128)S(1)} %get-tuple-element.4.joined, f32[2,16,16,128]{3,2,1,0:T(8,128)S(1)} %get-tuple-element.5.restored), custom_call_target="tpu_custom_call" | custom-call | tf_op jit(solution)/shard_map/pallas_call | solution.py:488
